TPU v7x, 128 devices: a whole 4x4x4 slice. The times are simulated.
128 devices in a mesh: gx: 16 (over y, z), gy: 8 (over x, core).
Axes of the slice: x: 4, y: 4, z: 4, core: 2. Of those that a mesh axis runs over, the one named last changes fastest.
Arguments:
- feats: bfloat16 [16, 8, 16, 512, 128], P('gx', 'gy'), may hold values from -6 to 6
- voxel_mask: int32 [16, 8, 16, 512], P('gx', 'gy'), may hold values 0 or 1
- brick_coord: int32 [16, 8, 16, 3], P('gx', 'gy'), may hold values from 0 to 3, as said below
- brick_count: int32 [16, 8, 2], P('gx', 'gy'), may hold values from 5 to 8, as said below
- route: int32 [16, 8, 16, 2], P('gx', 'gy'), may hold values from 0 to 15, as said below
- conv_weight: bfloat16 [3456, 128], replicated, may hold values from -0.109375 to 0.109375
- down_weight: bfloat16 [1024, 128], replicated, may hold values from -0.1875 to 0.1875
- coarse_grad: bfloat16 [16, 8, 32, 64, 128], P('gx', 'gy'), may hold values from -24 to 24
Outputs:
- coarse: bfloat16 [16, 8, 32, 64, 128], P('gx', 'gy')
- feat_grad: bfloat16 [16, 8, 16, 512, 128], P('gx', 'gy')
- conv_grad: float32 [3456, 128], replicated
- down_grad: float32 [1024, 128], replicated
Inputs may be any that keep to these rules, and one draw needn't show every extreme that they name: `brick_coord`: each slot names a brick position inside its device's tile of 4 x 4 x 4 bricks. The first 8 slots of a device hold distinct positions in the tile's outer brick columns (x or y equal to 0 or 3); the other slots hold distinct positions in the inner columns. `brick_count`: occupied slots come first in each half; some device has all its slots occupied. `route`: all slots of one device have distinct pairs (owner, place), so a device sends at most 2 sub-bricks to one owner; in every gy row one owner receives 2 sub-bricks from every device of the row.
All inputs are finite; a program needn't handle non-finite values. No bound on the sum of `voxel_mask` on one device may be relied on, other than what follows from the above.
Results may differ from a plain program's by a relative error of at most 0.005.
Values may be sent and summed in bfloat16 or wider, within the bound.
No kernel may reach another device: no remote copies, remote signals or barrier semaphores. Data moves between devices by JAX's collectives and lax.ppermute only.
A program may use at most 256 MiB of HBM per device.

v0:
```python
import math

import jax
import jax.numpy as jnp
import numpy as np
from jax import lax
from jax.sharding import PartitionSpec as P

CH = 128
EDGE = 8
VOX = 512
TILE = 4
SLOTS = 16
BORDER = 8
CAP = 2


def with_halo(cells, sides, width):
    for axis, dim in sides:
        count = lax.axis_size(axis)
        ends = count - 1
        head = lax.slice_in_dim(cells, 0, width, axis=dim)
        tail = lax.slice_in_dim(cells, cells.shape[dim] - width, cells.shape[dim], axis=dim)
        cells = jnp.concatenate(
            [
                lax.ppermute(tail, axis, [(i, (i + 1) % count) for i in range(ends)]),
                cells,
                lax.ppermute(head, axis, [((i + 1) % count, i) for i in range(ends)]),
            ],
            axis=dim,
        )
    return cells


def tap_offsets():
    return np.array(
        [[a - 1, b - 1, c - 1] for a in range(3) for b in range(3) for c in range(3)],
        dtype=np.int32,
    )


def padded_volume(brick_pool, neighbour_index):
    count = brick_pool.shape[0]
    width = brick_pool.shape[-1]
    voxels = brick_pool.reshape(count, EDGE, EDGE, EDGE, width)
    ranges = [(EDGE - 1, EDGE), (0, EDGE), (0, 1)]
    planes = []
    for a in range(3):
        lines = []
        for b in range(3):
            pieces = []
            for c in range(3):
                sliced = voxels[
                    :,
                    ranges[a][0] : ranges[a][1],
                    ranges[b][0] : ranges[b][1],
                    ranges[c][0] : ranges[c][1],
                ]
                pieces.append(jnp.take(sliced, neighbour_index[:, 9 * a + 3 * b + c], axis=0))
            lines.append(jnp.concatenate(pieces, axis=3))
        planes.append(jnp.concatenate(lines, axis=2))
    return jnp.concatenate(planes, axis=1)


def window_rows(padded, tap):
    a = tap // 9
    b = tap // 3 % 3
    c = tap % 3
    count = padded.shape[0]
    width = padded.shape[-1]
    return padded[:, a : a + EDGE, b : b + EDGE, c : c + EDGE].reshape(count * EDGE**3, width)


def convolve(padded, weight):
    total = None
    for tap in range(27):
        term = jnp.dot(
            window_rows(padded, tap),
            weight[tap * CH : (tap + 1) * CH],
            preferred_element_type=jnp.float32,
        )
        total = term if total is None else total + term
    return total


def pool_pairs(activated):
    count = activated.shape[0]
    half = EDGE // 2
    blocks = activated.reshape(count, half, 2, half, 2, half, 2, CH).transpose(
        0, 1, 3, 5, 2, 4, 6, 7
    )
    return blocks.reshape(count * half**3, 8 * CH)


def unpool_pairs(columns, count):
    half = EDGE // 2
    blocks = columns.reshape(count, half, half, half, 2, 2, 2, CH).transpose(0, 1, 4, 2, 5, 3, 6, 7)
    return blocks.reshape(count, VOX, CH)


def per_device(
    feats, voxel_mask, brick_coord, brick_count, route, conv_weight, down_weight, coarse_grad
):
    tiles_x = lax.axis_size("gx")
    tiles_y = lax.axis_size("gy")
    quarter = VOX // 8
    beside_all = np.array([0, 1, 2, 3, 5, 6, 7, 8], dtype=np.int32)
    slot_ids = jnp.arange(SLOTS, dtype=jnp.int32)
    counts = brick_count[0, 0]
    occupied = jnp.where(slot_ids < BORDER, slot_ids < counts[0], slot_ids - BORDER < counts[1])
    active = voxel_mask[0, 0].astype(jnp.float32) * occupied.astype(jnp.float32)[:, None]
    inputs = feats[0, 0] * active.astype(jnp.bfloat16)[:, :, None]
    coords = brick_coord[0, 0]
    labels = jnp.where(
        occupied, 1 + coords[:, 0] + TILE * coords[:, 1] + TILE * TILE * coords[:, 2], 0
    )[:BORDER]
    outgoing = inputs[:BORDER]
    arrived, arrived_labels = (
        with_halo(outgoing[None, None], (("gx", 0), ("gy", 1)), 1),
        with_halo(labels.astype(jnp.bfloat16)[None, None], (("gx", 0), ("gy", 1)), 1),
    )
    remote = arrived.reshape(9, BORDER, -1, CH)[beside_all].reshape(8 * BORDER, -1, CH)
    remote_labels = arrived_labels.reshape(9, BORDER)[beside_all].astype(jnp.int32)
    packed = remote_labels - 1
    shift_x = jnp.asarray(beside_all // 3 - 1) * TILE
    shift_y = jnp.asarray(beside_all % 3 - 1) * TILE
    far_x = packed % TILE + shift_x[:, None]
    far_y = packed // TILE % TILE + shift_y[:, None]
    far_z = packed // (TILE * TILE)
    cand_x = jnp.concatenate([coords[:, 0], far_x.reshape(-1)])
    cand_y = jnp.concatenate([coords[:, 1], far_y.reshape(-1)])
    cand_z = jnp.concatenate([coords[:, 2], far_z.reshape(-1)])
    cand_live = jnp.concatenate([occupied, (remote_labels > 0).reshape(-1)])
    offsets = jnp.asarray(tap_offsets())
    wanted = coords[:, None, :] + offsets[None]
    matches = (
        (wanted[..., 0:1] == cand_x)
        & (wanted[..., 1:2] == cand_y)
        & (wanted[..., 2:3] == cand_z)
        & cand_live
    )
    cand_total = cand_x.shape[0]
    neighbour_index = jnp.sum(
        jnp.where(matches, jnp.arange(cand_total, dtype=jnp.int32), 0), axis=2
    )
    neighbour_index = neighbour_index + jnp.where(jnp.any(matches, axis=2), 0, cand_total)
    empty_brick = jnp.zeros((1, VOX, CH), jnp.bfloat16)
    brick_pool = jnp.concatenate([inputs, remote, empty_brick], axis=0)
    input_padded = padded_volume(brick_pool, neighbour_index)
    preact = convolve(input_padded, conv_weight).reshape(SLOTS, VOX, CH)
    activated = (jax.nn.silu(preact) * active[..., None]).astype(jnp.bfloat16)
    block_rows = pool_pairs(activated)
    sub_rows = jnp.dot(block_rows, down_weight, preferred_element_type=jnp.float32).astype(
        jnp.bfloat16
    )
    sub_rows = sub_rows.reshape(SLOTS, quarter * CH)
    received_count = CAP * tiles_x
    target = jnp.where(occupied, route[0, 0, :, 0] * CAP + route[0, 0, :, 1], -1)
    placing = (target[None, :] == jnp.arange(received_count, dtype=jnp.int32)[:, None]).astype(
        jnp.bfloat16
    )
    sending = jnp.dot(placing, sub_rows, preferred_element_type=jnp.float32).astype(jnp.bfloat16)
    coarse_block = lax.all_to_all(
        sending.reshape(tiles_x, CAP, quarter * CH), "gx", split_axis=0, concat_axis=0, tiled=True
    ).reshape(received_count, quarter * CH)
    coarse = coarse_block.reshape(1, 1, received_count, quarter, CH)
    returned = lax.all_to_all(
        coarse_grad[0, 0].reshape(tiles_x, CAP, quarter * CH),
        "gx",
        split_axis=0,
        concat_axis=0,
        tiled=True,
    )
    returned = returned.reshape(received_count, quarter * CH)
    grad_rows = lax.dot_general(
        placing, returned, (((0,), (0,)), ((), ())), preferred_element_type=jnp.float32
    ).astype(jnp.bfloat16)
    grad_rows = grad_rows.reshape(SLOTS * quarter, CH)
    down_local = lax.dot_general(
        block_rows, grad_rows, (((0,), (0,)), ((), ())), preferred_element_type=jnp.float32
    )
    back_rows = jnp.dot(grad_rows, down_weight.T, preferred_element_type=jnp.float32)
    grad_act = unpool_pairs(back_rows, SLOTS)
    sigmoid_z = jax.nn.sigmoid(preact)
    grad_pre = (
        grad_act * active[..., None] * sigmoid_z * (1.0 + preact * (1.0 - sigmoid_z))
    ).astype(jnp.bfloat16)
    grad_out = grad_pre[:BORDER]
    grad_arrived = with_halo(grad_out[None, None], (("gx", 0), ("gy", 1)), 1)
    grad_remote = grad_arrived.reshape(9, BORDER, -1, CH)[beside_all].reshape(8 * BORDER, -1, CH)
    grad_pool = jnp.concatenate([grad_pre, grad_remote, empty_brick], axis=0)
    grad_padded = padded_volume(grad_pool, neighbour_index)
    flipped = conv_weight.reshape(27, CH, CH)[::-1].transpose(0, 2, 1).reshape(27 * CH, CH)
    grad_flat = grad_pre.reshape(SLOTS * VOX, CH)
    tap_grads = [
        lax.dot_general(
            window_rows(input_padded, tap),
            grad_flat,
            (((0,), (0,)), ((), ())),
            preferred_element_type=jnp.float32,
        )
        for tap in range(27)
    ]
    conv_local = jnp.concatenate(tap_grads, axis=0)
    back_all = convolve(grad_padded, flipped).reshape(SLOTS, VOX, CH)
    feat_grad = (back_all * active[..., None]).astype(jnp.bfloat16)[None, None]
    conv_sum, down_sum = lax.psum((conv_local, down_local), ("gx", "gy"))
    total_slots = tiles_x * tiles_y * SLOTS
    conv_grad = conv_sum * (1.0 / math.sqrt(total_slots * VOX))
    down_grad = down_sum * (1.0 / math.sqrt(total_slots * VOX // 8))
    return (coarse, feat_grad, conv_grad, down_grad)


def solution(mesh):
    in_specs = (
        P("gx", "gy", None, None, None),
        P("gx", "gy", None, None),
        P("gx", "gy", None, None),
        P("gx", "gy", None),
        P("gx", "gy", None, None),
        P(),
        P(),
        P("gx", "gy", None, None, None),
    )
    out_specs = (P("gx", "gy", None, None, None), P("gx", "gy", None, None, None), P(), P())
    return jax.shard_map(
        per_device, mesh=mesh, in_specs=in_specs, out_specs=out_specs, check_vma=False
    )
```

profile of v0, /device:TPU:1, one launch (start us, length us, event | category | flops | bytes accessed | tf_op | source)
XLA Modules:
  0.0 944.7 jit_solution(12684118593765620161)
XLA Ops:
  30.2 8.0 all-to-all-start.1
  117.3 9.0 pad_maximum_fusion
  126.4 8.5 gather_fusion
  134.9 16.5 %copy.431 = bf16[64,8,8,8,128]{4,0,3,2,1:T(8,128)(2,1)} copy(bf16[64,8,8,8,128]{4,3,2,1,0:T(8,128)(2,1)} %bitcast.661) | data formatting | bytes 16777216 | tf_op jit(solution)/shard_map/concatenate | solution.py:148
  151.4 7.8 maximum_maximum_fusion
  160.2 7.3 copy.450
  200.5 6.3 gather_fusion.16
  250.5 7.8 maximum_maximum_fusion.7
  258.4 6.2 maximum_maximum_fusion.3
  264.6 18.8 %fusion.47 = (bf16[16,8,8,8,128]{4,3,2,1,0:T(8,128)(2,1)}, bf16[16,8,8,8,128]{4,3,2,1,0:T(8,128)(2,1)}, bf16[16,8,8,8,128]{4,3,2,1,0:T(8,128)(2,1)}, bf16[16,8,8...) fusion(bf16[16,9,10,10,128]{4,3,2,1,0:T(8,128)(2,1)} %maximum_m, ...), kind=kLoop, calls=%fused_computation.507 | loop fusion | bytes 37748736 | tf_op jit(solution)/shard_map/slice | solution.py:71
  283.5 7.8 fusion.52
  330.0 6.4 maximum_maximum_fusion.2
  336.4 18.7 %fusion.48 = (bf16[16,8,8,8,128]{4,3,2,1,0:T(8,128)(2,1)}, bf16[16,8,8,8,128]{4,3,2,1,0:T(8,128)(2,1)}, bf16[16,8,8,8,128]{4,3,2,1,0:T(8,128)(2,1)}, bf16[16,8,8...) fusion(bf16[16,9,10,10,128]{4,3,2,1,0:T(8,128)(2,1)} %maximum_m, ...), kind=kLoop, calls=%fused_computation.508 | loop fusion | bytes 37748736 | tf_op jit(solution)/shard_map/slice | solution.py:71
  357.4 7.9 fusion.51
  410.3 6.3 exponential_add_fusion
  490.5 6.8 all-to-all-start
  497.3 6.1 multiply_convert_fusion.2
  503.4 6.4 all-to-all-done
  512.1 130.9 %all-reduce.3.cloned.1.call-done = (f32[3456,128]{1,0:T(8,128)}, f32[1024,128]{1,0:T(8,128)}) async-done(((f32[3456,128]{1,0:T(8,128)}, f32[1024,128]{1,0:T(8,128)}), (f32[3456,128]{1,0:T(8,128)}, f32[1024,128]{1,0:T(8,128)})) %all-reduce.3.cloned.1.call-update) | async-done | bytes 2293776 | tf_op jit(solution)/shard_map/psum | solution.py:207
  647.7 8.6 pad_maximum_fusion.1
  656.2 9.9 %copy.486 = bf16[3,3,8,512,128]{4,3,2,1,0:T(8,128)(2,1)} copy(bf16[3,3,8,512,128]{4,2,3,1,0:T(8,128)(2,1)} %pad_maximum_fusion.1) | data formatting | bytes 18874368 | tf_op jit(solution)/shard_map/concatenate | solution.py:24
  666.1 8.9 gather_fusion.2
  675.1 16.5 %copy.487 = bf16[64,8,8,8,128]{4,0,3,2,1:T(8,128)(2,1)} copy(bf16[64,8,8,8,128]{4,3,2,1,0:T(8,128)(2,1)} %bitcast.660) | data formatting | bytes 16777216 | tf_op jit(solution)/shard_map/concatenate | solution.py:191
  691.5 7.6 maximum_maximum_fusion.1
  701.4 7.5 copy.506
  720.1 6.3 gather_fusion.43
  785.4 7.8 maximum_maximum_fusion.9
  793.3 6.2 maximum_maximum_fusion.5
  799.5 18.7 %fusion.45 = (bf16[16,8,8,8,128]{4,3,2,1,0:T(8,128)(2,1)}, bf16[16,8,8,8,128]{4,3,2,1,0:T(8,128)(2,1)}, bf16[16,8,8,8,128]{4,3,2,1,0:T(8,128)(2,1)}, bf16[16,8,8...) fusion(bf16[16,9,10,10,128]{4,3,2,1,0:T(8,128)(2,1)} %maximum_m, ...), kind=kLoop, calls=%fused_computation.505 | loop fusion | bytes 37748736 | tf_op jit(solution)/shard_map/slice | solution.py:71
  818.2 7.8 fusion.50
  865.6 6.2 maximum_maximum_fusion.4
  871.8 18.9 %fusion.46 = (bf16[16,8,8,8,128]{4,3,2,1,0:T(8,128)(2,1)}, bf16[16,8,8,8,128]{4,3,2,1,0:T(8,128)(2,1)}, bf16[16,8,8,8,128]{4,3,2,1,0:T(8,128)(2,1)}, bf16[16,8,8...) fusion(bf16[16,9,10,10,128]{4,3,2,1,0:T(8,128)(2,1)} %maximum_m, ...), kind=kLoop, calls=%fused_computation.506 | loop fusion | bytes 37748736 | tf_op jit(solution)/shard_map/slice | solution.py:71
  (667 shorter events, 504.2 us)
Async XLA Ops:
  7.2 94.1 %copy-start = (bf16[1024,128]{1,0:T(8,128)(2,1)S(1)}, bf16[1024,128]{1,0:T(8,128)(2,1)}, u32[]{:S(2)}) copy-start(bf16[1024,128]{1,0:T(8,128)(2,1)} %param.37) | copy-start | bytes 786436
  12.3 44.8 %collective-permute-start.4 = (bf16[1,1,8]{2,1,0:T(2,128)(2,1)}, bf16[1,1,8]{2,1,0:T(2,128)(2,1)}, u32[]{:S(2)}, u32[]{:S(2)}) collective-permute-start(bf16[1,1,8]{2,1,0:T(2,128)(2,1)} %slice_bitcast_fusion.136), channel_id=1, source_target_pairs={{0,8},{8,16},{16,24},{24,32},{32,40},{40,48},{48,56},{56,64},{64,7... | collective-permute-start | bytes 56 | tf_op jit(solution)/shard_map/ppermute | solution.py:26
  17.3 39.8 %collective-permute-start.5 = (bf16[1,1,8]{2,1,0:T(2,128)(2,1)}, bf16[1,1,8]{2,1,0:T(2,128)(2,1)}, u32[]{:S(2)}, u32[]{:S(2)}) collective-permute-start(bf16[1,1,8]{2,1,0:T(2,128)(2,1)} %slice_bitcast_fusion.136), channel_id=1, source_target_pairs={{8,0},{16,8},{24,16},{32,24},{40,32},{48,40},{56,48},{64,56},{72,6... | collective-permute-start | bytes 56 | tf_op jit(solution)/shard_map/ppermute | solution.py:28
  20.1 18.9 %copy-start.100 = (s32[1,1,16,512]{3,2,1,0:T(8,128)S(1)}, s32[1,1,16,512]{3,2,1,0:T(8,128)}, u32[]{:S(2)}) copy-start(s32[1,1,16,512]{3,2,1,0:T(8,128)} %param.32) | copy-start | bytes 98308
  20.1 19.5 %copy-start.72 = (bf16[1,1,16,512,128]{4,3,2,1,0:T(8,128)(2,1)S(1)}, bf16[1,1,16,512,128]{4,3,2,1,0:T(8,128)(2,1)}, u32[]{:S(2)}) copy-start(bf16[1,1,16,512,128]{4,3,2,1,0:T(8,128)(2,1)} %param.31) | copy-start | bytes 6291460
  22.0 50.9 %collective-permute-start = (bf16[1,1,8,512,128]{4,3,2,1,0:T(8,128)(2,1)S(1)}, bf16[1,1,8,512,128]{4,3,2,1,0:T(8,128)(2,1)}, u32[]{:S(2)}, u32[]{:S(2)}) collective-permute-start(bf16[1,1,8,512,128]{4,3,2,1,0:T(8,128)(2,1)S(1)} %fusion.5), channel_id=1, source_target_pairs={{0,8},{8,16},{16,24},{24,32},{32,40},{40,48},{48,56},{56,64},{64,7... | collective-permute-start | bytes 3145736 | tf_op jit(solution)/shard_map/ppermute | solution.py:26
  27.0 45.9 %collective-permute-start.1 = (bf16[1,1,8,512,128]{4,3,2,1,0:T(8,128)(2,1)S(1)}, bf16[1,1,8,512,128]{4,3,2,1,0:T(8,128)(2,1)}, u32[]{:S(2)}, u32[]{:S(2)}) collective-permute-start(bf16[1,1,8,512,128]{4,3,2,1,0:T(8,128)(2,1)S(1)} %fusion.5), channel_id=1, source_target_pairs={{8,0},{16,8},{24,16},{32,24},{40,32},{48,40},{56,48},{64,56},{72,6... | collective-permute-start | bytes 3145736 | tf_op jit(solution)/shard_map/ppermute | solution.py:28
  30.2 63.4 %all-to-all-start.1 = ((bf16[16,2,8192]{2,1,0:T(2,128)(2,1)}), bf16[16,2,8192]{2,1,0:T(2,128)(2,1)}, u32[]{:S(2)}, u32[]{:S(2)}) async-start(bf16[16,2,8192]{2,1,0:T(2,128)(2,1)} %reshape_squeeze.3), calls=%async_computation.1 | async-start | bytes 1048576 | tf_op jit(solution)/shard_map/all_to_all | solution.py:167
  38.3 604.7 %all-reduce.3.cloned.1.call-start = ((), (), s32[]{:S(2)}) async-start(), calls=%async_computation.2 | async-start | bytes 4587520 | tf_op jit(solution)/shard_map/psum | solution.py:207
  56.5 94.9 %copy-start.142 = (bf16[81]{0:T(256)(128)(2,1)}, bf16[81]{0:T(256)(128)(2,1)S(1)}, u32[]{:S(2)}) copy-start(bf16[81]{0:T(256)(128)(2,1)S(1)} %pad.115.clone) | copy-start | bytes 490
  57.8 7.0 collective-permute-start.6
  62.9 4.9 collective-permute-start.7
  72.9 22.7 %copy-start.140 = (s32[16]{0:T(128)S(1)}, s32[16]{0:T(128)}, u32[]{:S(2)}) copy-start(s32[16]{0:T(128)} %get-tuple-element.12) | copy-start | bytes 196
  76.5 36.5 %collective-permute-start.2 = (bf16[3,1,8,512,128]{4,3,2,1,0:T(8,128)(2,1)}, bf16[3,1,8,512,128]{4,3,2,1,0:T(8,128)(2,1)}, u32[]{:S(2)}, u32[]{:S(2)}) collective-permute-start(bf16[3,1,8,512,128]{4,3,2,1,0:T(8,128)(2,1)} %pad_maximum_fusion.2), channel_id=1, source_target_pairs={{0,1},{1,2},{2,3},{3,4},{4,5},{5,6},{6,7},{8,9},{9,10},{10,11},{11... | collective-permute-start | bytes 9437192 | tf_op jit(solution)/shard_map/ppermute | solution.py:26
  78.4 38.9 %collective-permute-start.3 = (bf16[3,1,8,512,128]{4,3,2,1,0:T(8,128)(2,1)}, bf16[3,1,8,512,128]{4,3,2,1,0:T(8,128)(2,1)}, u32[]{:S(2)}, u32[]{:S(2)}) collective-permute-start(bf16[3,1,8,512,128]{4,3,2,1,0:T(8,128)(2,1)} %pad_maximum_fusion.2), channel_id=1, source_target_pairs={{1,0},{2,1},{3,2},{4,3},{5,4},{6,5},{7,6},{9,8},{10,9},{11,10},{12... | collective-permute-start | bytes 9437192 | tf_op jit(solution)/shard_map/ppermute | solution.py:28
  208.6 174.9 %copy-start.2 = (bf16[16,8,8,8,128]{4,3,2,1,0:T(8,128)(2,1)}, bf16[16,8,8,8,128]{4,3,2,1,0:T(8,128)(2,1)S(1)}, u32[]{:S(2)}) copy-start(bf16[16,8,8,8,128]{4,3,2,1,0:T(8,128)(2,1)S(1)} %broadcast_select_fusion.1) | copy-start | bytes 6291460
  208.7 18.2 %copy-start.113 = (pred[16]{0:T(512)(128)(4,1)S(1)}, pred[16]{0:T(512)(128)(4,1)}, u32[]{:S(2)}) copy-start(pred[16]{0:T(512)(128)(4,1)} %get-tuple-element.205) | copy-start | bytes 52
  208.7 21.1 %copy-start.111 = (pred[16]{0:T(512)(128)(4,1)S(1)}, pred[16]{0:T(512)(128)(4,1)}, u32[]{:S(2)}) copy-start(pred[16]{0:T(512)(128)(4,1)} %get-tuple-element.211) | copy-start | bytes 52
  208.7 24.7 %copy-start.95 = (bf16[81,128]{1,0:T(8,128)(2,1)S(1)}, bf16[81,128]{1,0:T(8,128)(2,1)}, u32[]{:S(2)}) copy-start(bf16[81,128]{1,0:T(8,128)(2,1)} %get-tuple-element.104) | copy-start | bytes 62212
  208.7 32.3 %copy-start.110 = (pred[16]{0:T(512)(128)(4,1)S(1)}, pred[16]{0:T(512)(128)(4,1)}, u32[]{:S(2)}) copy-start(pred[16]{0:T(512)(128)(4,1)} %get-tuple-element.209) | copy-start | bytes 52
  293.5 27.2 %copy-start.131 = (pred[16]{0:T(512)(128)(4,1)S(1)}, pred[16]{0:T(512)(128)(4,1)}, u32[]{:S(2)}) copy-start(pred[16]{0:T(512)(128)(4,1)} %get-tuple-element.227) | copy-start | bytes 52
  336.4 18.7 %copy-start.76 = (bf16[3456,128]{1,0:T(8,128)(2,1)S(1)}, bf16[3456,128]{1,0:T(8,128)(2,1)}, u32[]{:S(2)}) copy-start(bf16[3456,128]{1,0:T(8,128)(2,1)} %param.36) | copy-start | bytes 2654212
  410.3 42.4 %copy-start.4 = (f32[8192,128]{1,0:T(8,128)}, f32[8192,128]{1,0:T(8,128)S(1)}, u32[]{:S(2)}) copy-start(f32[8192,128]{1,0:T(8,128)S(1)} %get-tuple-element.251) | copy-start | bytes 12582916
  419.9 51.5 %collective-permute-start.8 = (bf16[1,1,8,512,128]{4,2,3,1,0:T(8,128)(2,1)S(1)}, bf16[1,1,8,512,128]{4,2,3,1,0:T(8,128)(2,1)}, u32[]{:S(2)}, u32[]{:S(2)}) collective-permute-start(bf16[1,1,8,512,128]{4,2,3,1,0:T(8,128)(2,1)S(1)} %fusion.6), channel_id=1, source_target_pairs={{0,8},{8,16},{16,24},{24,32},{32,40},{40,48},{48,56},{56,64},{64,7... | collective-permute-start | bytes 3145736 | tf_op jit(solution)/shard_map/ppermute | solution.py:26
  424.4 47.0 %collective-permute-start.9 = (bf16[1,1,8,512,128]{4,2,3,1,0:T(8,128)(2,1)S(1)}, bf16[1,1,8,512,128]{4,2,3,1,0:T(8,128)(2,1)}, u32[]{:S(2)}, u32[]{:S(2)}) collective-permute-start(bf16[1,1,8,512,128]{4,2,3,1,0:T(8,128)(2,1)S(1)} %fusion.6), channel_id=1, source_target_pairs={{8,0},{16,8},{24,16},{32,24},{40,32},{48,40},{56,48},{64,56},{72,6... | collective-permute-start | bytes 3145736 | tf_op jit(solution)/shard_map/ppermute | solution.py:28
  475.2 172.5 %collective-permute-start.10 = (bf16[3,1,8,512,128]{4,2,3,1,0:T(8,128)(2,1)}, bf16[3,1,8,512,128]{4,2,3,1,0:T(8,128)(2,1)}, u32[]{:S(2)}, u32[]{:S(2)}) collective-permute-start(bf16[3,1,8,512,128]{4,2,3,1,0:T(8,128)(2,1)} %pad_maximum_fusion.3), channel_id=1, source_target_pairs={{0,1},{1,2},{2,3},{3,4},{4,5},{5,6},{6,7},{8,9},{9,10},{10,11},{11... | collective-permute-start | bytes 9437192 | tf_op jit(solution)/shard_map/ppermute | solution.py:26
  477.2 170.5 %collective-permute-start.11 = (bf16[3,1,8,512,128]{4,2,3,1,0:T(8,128)(2,1)}, bf16[3,1,8,512,128]{4,2,3,1,0:T(8,128)(2,1)}, u32[]{:S(2)}, u32[]{:S(2)}) collective-permute-start(bf16[3,1,8,512,128]{4,2,3,1,0:T(8,128)(2,1)} %pad_maximum_fusion.3), channel_id=1, source_target_pairs={{1,0},{2,1},{3,2},{4,3},{5,4},{6,5},{7,6},{9,8},{10,9},{11,10},{12... | collective-permute-start | bytes 9437192 | tf_op jit(solution)/shard_map/ppermute | solution.py:28
  490.5 19.4 %all-to-all-start = ((bf16[16,2,8192]{2,1,0:T(2,128)(2,1)}), bf16[16,2,8192]{2,1,0:T(2,128)(2,1)}, u32[]{:S(2)}, u32[]{:S(2)}) async-start(bf16[16,2,8192]{2,1,0:T(2,128)(2,1)} %reshape.576), calls=%async_computation | async-start | bytes 1048576 | tf_op jit(solution)/shard_map/all_to_all | solution.py:163
  737.8 16.9 %copy-start.116 = (pred[16]{0:T(512)(128)(4,1)S(1)}, pred[16]{0:T(512)(128)(4,1)}, u32[]{:S(2)}) copy-start(pred[16]{0:T(512)(128)(4,1)} %get-tuple-element.193) | copy-start | bytes 52
  740.6 18.0 %copy-start.114 = (pred[16]{0:T(512)(128)(4,1)S(1)}, pred[16]{0:T(512)(128)(4,1)}, u32[]{:S(2)}) copy-start(pred[16]{0:T(512)(128)(4,1)} %get-tuple-element.205) | copy-start | bytes 52
  740.6 21.0 %copy-start.112 = (pred[16]{0:T(512)(128)(4,1)S(1)}, pred[16]{0:T(512)(128)(4,1)}, u32[]{:S(2)}) copy-start(pred[16]{0:T(512)(128)(4,1)} %get-tuple-element.211) | copy-start | bytes 52
  834.6 21.7 %copy-start.132 = (pred[16]{0:T(512)(128)(4,1)S(1)}, pred[16]{0:T(512)(128)(4,1)}, u32[]{:S(2)}) copy-start(pred[16]{0:T(512)(128)(4,1)} %get-tuple-element.227) | copy-start | bytes 52
  (132 other events, 593.9 us)
Sparse Core Ops, SparseCore 0:
  488.6 154.3 all-reduce.2
where the time goes:
time: 960 us; the launch traced here: 945 us
  local copies, waits for them, and re-layouts  446 us (46%)
  other arithmetic  201 us (21%)
  waiting for transfers between devices  148 us (15%)
  matrix products  80.5 us (8%)
  starting transfers between devices  52.8 us (6%)
  between operations  16.1 us (2%)
    psum x1, waiting for transfers between devices, per_device(): conv_sum, down_sum = lax.psum((conv_local, down_local), ('gx', 'gy'))  131 us
    gather x54, local copies, waits for them, and re-layouts, padded_volume(): jnp.take(sliced, neighbour_index[:, 9 * a + 3 * b + c], axis=0)  105 us
    slice x8, local copies, waits for them, and re-layouts, window_rows(): padded[:, a:a + EDGE, b:b + EDGE, c:c + EDGE]  104 us
    another operation x50, local copies, waits for them, and re-layouts, padded_volume(): jnp.take(sliced, neighbour_index[:, 9 * a + 3 * b + c], axis=0)  64.6 us
    unnamed x303, local copies, waits for them, and re-layouts  57.3 us
    select_n x54, other arithmetic, padded_volume(): jnp.take(sliced, neighbour_index[:, 9 * a + 3 * b + c], axis=0)  52.1 us
    dot_general x54, matrix products, convolve(): jnp.dot(window_rows(padded, tap), weight[tap * CH:(tap + 1) * CH], prefer...  45.8 us
    concatenate x6, other arithmetic, with_halo(): jnp.concatenate([lax.ppermute(tail, axis, [(i, (i + 1) % count) for i in...  26.4 us
  transfers between devices with their start and end apart: 15, of which 5 were waited for; matrix products, arithmetic and copies ran while one was open for 12% of the time, Pallas kernels for 0%

commit v1 on v0

v1 whole, which is shorter than its diff:
```python
import math

import jax
import jax.numpy as jnp
import numpy as np
from jax import lax
from jax.experimental import pallas as pl
from jax.experimental.pallas import tpu as pltpu
from jax.sharding import PartitionSpec as P

CH = 128
EDGE = 8
VOX = 512
TILE = 4
SLOTS = 16
BORDER = 8
CAP = 2
BF = jnp.bfloat16
F32 = jnp.float32
FACE = 64 * BORDER
LAB = 16
XMSG = FACE + LAB
YMSG = XMSG + 2 * 64 + 2 * LAB
SHARD = 40
VSTEP = 4096
NOWHERE = -(1 << 20)


def position_code(x, y, z):
    return (x + TILE) * 96 + (y + TILE) * 8 + z + 1


def label_code(row, shift_x, shift_y):
    packed = row.astype(F32).astype(jnp.int32) - 1
    code = position_code(
        (packed & 3) + shift_x * TILE, ((packed >> 2) & 3) + shift_y * TILE, packed >> 4
    )
    return jnp.where(packed < 0, NOWHERE, code)


def one_hot(left, right):
    return jnp.where(left == right, 1.0, 0.0).astype(BF)


def tap_delta(a, b, c):
    return (a - 1) * 96 + (b - 1) * 8 + (c - 1)


def lane_row():
    return lax.broadcasted_iota(jnp.int32, (1, 128), 1)


def tile_at(vol, xp, yp, zp):
    return vol[xp, yp, zp // 2, :, (zp % 2) * CH : (zp % 2 + 1) * CH]


def put_tile(vol, xp, yp, zp, value):
    vol[xp, yp, zp // 2, :, (zp % 2) * CH : (zp % 2 + 1) * CH] = value


def fill_halo(vol, sel, meta, left, right, lower, upper):
    base = meta[0:SLOTS]
    lane = lane_row()
    own = meta[2 * SLOTS : 2 * SLOTS + 1] + VSTEP * (lane // SLOTS)
    nothing = jnp.zeros((SLOTS, 128), BF)
    zs = [7, 0, 1, 2, 3, 4, 5, 6, 7, 0]
    cs = [0] + [1] * 8 + [2]

    sides = [
        (0, 1, left, -1, 0),
        (2, 1, right, 1, 0),
        (1, 0, lower, 0, -1),
        (1, 2, upper, 0, 1),
    ]
    for a, b, msg, sx, sy in sides:
        far = label_code(msg[FACE : FACE + 1], sx, sy) + VSTEP * (lane // BORDER)
        for zp in range(10):
            for col in range(2):
                rows = pl.ds((zp * 2 + col) * SLOTS, SLOTS)
                want = base + (tap_delta(a, b, cs[zp]) + VSTEP * (col * 8 + zs[zp]))
                here = one_hot(want, own + VSTEP * 8 * col)
                sel[rows, col * 128 : (col + 1) * 128] = here
                sel[rows, (1 - col) * 128 : (2 - col) * 128] = nothing
                sel[rows, 256:384] = one_hot(want, far)
        for half in range(2):
            parts = []
            for k in range(2):
                first = (half * 2 + k) * 2
                tiles = []
                for col in range(2):
                    for z in range(8):
                        if b == 1:
                            tiles.append(tile_at(vol, 8 if a == 0 else 1, first + col + 1, z + 1))
                        else:
                            tiles.append(tile_at(vol, first + col + 1, 8 if b == 0 else 1, z + 1))
                tiles.append(msg[first * 64 : (first + 2) * 64])
                parts.append(jnp.concatenate(tiles, axis=0))
            data = jnp.concatenate(parts, axis=1)
            out = jnp.dot(sel[0:320, :], data, preferred_element_type=F32).astype(BF)
            for k in range(2):
                for zp in range(10):
                    for col in range(2):
                        at = (half * 2 + k) * 2 + col + 1
                        row = (zp * 2 + col) * SLOTS
                        value = out[row : row + SLOTS, k * 128 : (k + 1) * 128]
                        if b == 1:
                            put_tile(vol, 0 if a == 0 else 9, at, zp, value)
                        else:
                            put_tile(vol, at, 0 if b == 0 else 9, zp, value)

    for c in (0, 2):
        for v in range(16):
            rows = pl.ds(v * SLOTS, SLOTS)
            j = v // 8
            want = base + (tap_delta(1, 1, c) + VSTEP * v)
            sel[rows, j * 128 : (j + 1) * 128] = one_hot(want, own + VSTEP * 8 * j)
            sel[rows, (1 - j) * 128 : (2 - j) * 128] = nothing
        for half in range(2):
            parts = []
            for k in range(2):
                tiles = []
                for v in range(16):
                    at = (half * 2 + k) * 16 + v
                    tiles.append(tile_at(vol, at // 8 + 1, at % 8 + 1, 8 if c == 0 else 1))
                parts.append(jnp.concatenate(tiles, axis=0))
            data = jnp.concatenate(parts, axis=1)
            out = jnp.dot(sel[0:256, 0:256], data, preferred_element_type=F32).astype(BF)
            for k in range(2):
                for v in range(16):
                    at = (half * 2 + k) * 16 + v
                    put_tile(
                        vol,
                        at // 8 + 1,
                        at % 8 + 1,
                        0 if c == 0 else 9,
                        out[v * SLOTS : (v + 1) * SLOTS, k * 128 : (k + 1) * 128],
                    )

    for a in (0, 2):
        for b in (0, 2):
            side = left if a == 0 else right
            face = lower if b == 0 else upper
            side_code = label_code(side[FACE : FACE + 1], a - 1, 0)
            face_code = label_code(face[FACE : FACE + 1], 0, b - 1)
            corner_at = XMSG if a == 0 else XMSG + 64
            corner_lab = XMSG + 128 if a == 0 else XMSG + 128 + LAB
            corner_code = label_code(face[corner_lab : corner_lab + 1], a - 1, b - 1)
            voxel = VSTEP * (lane % 64 // BORDER)
            beside = jnp.where(lane < 64, side_code, face_code) + voxel
            across = jnp.where(lane < 64, corner_code, NOWHERE) + voxel
            for zp in range(10):
                rows = pl.ds(zp * SLOTS, SLOTS)
                want = base + (tap_delta(a, b, cs[zp]) + VSTEP * zs[zp])
                sel[rows, 0:128] = one_hot(want, own)
                sel[rows, 128:256] = one_hot(want, beside)
                sel[rows, 256:384] = one_hot(want, across)
            xs = 8 if a == 0 else 1
            ys = 8 if b == 0 else 1
            tiles = [tile_at(vol, xs, ys, z + 1) for z in range(8)]
            line_y = (7 if b == 0 else 0) * 64
            line_x = (7 if a == 0 else 0) * 64
            tiles.append(side[line_y : line_y + 64])
            tiles.append(face[line_x : line_x + 64])
            tiles.append(face[corner_at : corner_at + 64])
            tiles.append(jnp.zeros((64, CH), BF))
            data = jnp.concatenate(tiles, axis=0)
            out = jnp.dot(sel[0:160, :], data, preferred_element_type=F32).astype(BF)
            for zp in range(10):
                put_tile(
                    vol,
                    0 if a == 0 else 9,
                    0 if b == 0 else 9,
                    zp,
                    out[zp * SLOTS : (zp + 1) * SLOTS],
                )


def pair_weights(wide, block):
    zero = jnp.zeros((CH, CH), BF)
    for a in range(3):
        for b in range(3):
            w0, w1, w2 = (block(a, b, c) for c in range(3))
            k = (a * 3 + b) * 2
            wide[k * 256 : k * 256 + 128, 0:128] = w0
            wide[k * 256 : k * 256 + 128, 128:256] = zero
            wide[k * 256 + 128 : k * 256 + 256, 0:128] = w1
            wide[k * 256 + 128 : k * 256 + 256, 128:256] = w0
            wide[k * 256 + 256 : k * 256 + 384, 0:128] = w2
            wide[k * 256 + 256 : k * 256 + 384, 128:256] = w1
            wide[k * 256 + 384 : k * 256 + 512, 0:128] = zero
            wide[k * 256 + 384 : k * 256 + 512, 128:256] = w2


def window(vol, x0, nx, a, b, h):
    return vol[pl.ds(x0 + a, nx), b : b + EDGE, h : h + 4].reshape(nx * EDGE * 4 * SLOTS, 256)


def conv_rows(vol, wide, x0, nx):
    taps = [window(vol, x0, nx, k // 6, k // 2 % 3, k % 2) for k in range(18)]
    return jnp.dot(jnp.concatenate(taps, axis=1), wide[...], preferred_element_type=F32)


def arrange_kernel(feats, mask_rows, labels, vol, mask, xlo, xhi, ylo, yhi):
    r = lax.broadcasted_iota(jnp.int32, (256, 256), 0)
    k = lax.broadcasted_iota(jnp.int32, (256, 256), 1)
    order = one_hot((r % SLOTS) * 16 + r // SLOTS, k)
    ones = jnp.ones((256, CH), BF)

    def at_x(x, carry):
        for q in range(4):
            first = pl.multiple_of(x * 64 + q * 16, 16)
            data = feats[:, pl.ds(first, 16), :].reshape(256, CH)
            chosen = order * mask_rows[x, q : q + 1, :]
            out = jnp.dot(
                chosen, jnp.concatenate([data, ones], axis=1), preferred_element_type=F32
            )
            tiles = out.astype(BF).reshape(2, 8, SLOTS, 256)
            for y in range(2):
                for z in range(8):
                    put_tile(vol, x + 1, q * 2 + y + 1, z + 1, tiles[y, z, :, 0:CH])
                    mask[x, q * 2 + y, z // 2, :, (z % 2) * CH : (z % 2 + 1) * CH] = tiles[
                        y, z, :, CH : 2 * CH
                    ]
            outer = out[:, 0:CH].reshape(2, 8, SLOTS, CH)[:, :, 0:BORDER]

            @pl.when(x == 0)
            def _():
                xlo[q * 128 : (q + 1) * 128] = outer.reshape(128, CH).astype(BF)

            @pl.when(x == EDGE - 1)
            def _():
                xhi[q * 128 : (q + 1) * 128] = outer.reshape(128, CH).astype(BF)

            line = pl.ds(pl.multiple_of(x * 64, 64), 64)
            if q == 0:
                ylo[line] = outer[0].reshape(64, CH).astype(BF)
            if q == 3:
                yhi[line] = outer[1].reshape(64, CH).astype(BF)
        return carry

    lax.fori_loop(0, EDGE, at_x, 0)
    for face in (xlo, xhi, ylo, yhi):
        face[FACE:XMSG] = labels[...]


def forward_kernel(
    vol_in, mask, left, right, lower, upper, meta, weight, down, returned, labels,
    grad_vol, gxlo, gxhi, gylo, gyhi, sending, partial,
    vol, sel, wide, grad_t, route, spread, acts, subs,
):
    vol[...] = vol_in[...]
    pair_weights(wide, lambda a, b, c: weight[((a * 3 + b) * 3 + c) * CH :][:CH])
    fill_halo(vol, sel, meta, left, right, lower, upper)

    lane = lane_row()
    for b in range(16):
        for j in range(4):
            route[b * 16 : (b + 1) * 16, j * 128 : (j + 1) * 128] = one_hot(
                meta[SLOTS : 2 * SLOTS] * 16 + b, lane + 128 * j
            )
    block = lax.broadcasted_iota(jnp.int32, (16, 128), 0)
    for t in range(2 * SLOTS):
        for j in range(2):
            spread[t * 16 : (t + 1) * 16, j * 128 : (j + 1) * 128] = one_hot(
                block * 64 + t, meta[2 * SLOTS + 1 : 2 * SLOTS + 2] + 64 * (lane // 16 + 8 * j)
            )

    def at_hx(hx, carry):
        pre_all = conv_rows(vol, wide, 2 * hx, 2).reshape(2, 4, 2, 64, 256)
        first = pl.multiple_of(hx * 16, 16)
        grad_sub = jnp.dot(
            route[...],
            returned[:, pl.ds(first, 16), :].reshape(512, CH),
            preferred_element_type=F32,
        ).astype(BF)
        subs[pl.ds(pl.multiple_of(hx * 256, 256), 256)] = grad_sub
        grad_act = lax.dot_general(
            grad_sub, down[...], (((1,), (1,)), ((), ())), preferred_element_type=F32
        )
        total = None
        for px in range(2):
            for py in range(2):
                q = px * 2 + py
                x = 2 * hx + px
                pre = pre_all[px, :, py].reshape(256, 256)
                live = jnp.stack([mask[x, 2 * hy + py] for hy in range(4)]).reshape(256, 256)
                live = live.astype(F32)
                sig = jax.nn.sigmoid(pre)
                act = (pre * sig * live).astype(BF)
                acts[q, pl.ds(pl.multiple_of(hx * 256, 256), 256)] = act
                term = jnp.dot(
                    act, down[q * 256 : (q + 1) * 256], preferred_element_type=F32
                )
                total = term if total is None else total + term
                grad = (
                    grad_act[:, q * 256 : (q + 1) * 256]
                    * live
                    * sig
                    * (1.0 + pre * (1.0 - sig))
                )
                grad_b = grad.astype(BF)
                shaped = grad_b.reshape(4, 4, SLOTS, 256)
                outer = grad.reshape(4, 4, SLOTS, 256)[:, :, 0:BORDER]
                turned = grad_b.T
                for hy in range(4):
                    y = 2 * hy + py
                    for p in range(4):
                        put_tile(grad_vol, x + 1, y + 1, 2 * p + 1, shaped[hy, p, :, 0:CH])
                        put_tile(grad_vol, x + 1, y + 1, 2 * p + 2, shaped[hy, p, :, CH:256])
                    zs = jnp.stack(
                        [outer[hy, z // 2, :, (z % 2) * CH : (z % 2 + 1) * CH] for z in range(8)]
                    )
                    flat = zs.reshape(64, CH).astype(BF)
                    if px == 0:
                        @pl.when(hx == 0)
                        def _():
                            gxlo[y * 64 : (y + 1) * 64] = flat
                    else:
                        @pl.when(hx == 3)
                        def _():
                            gxhi[y * 64 : (y + 1) * 64] = flat
                    line = pl.ds(pl.multiple_of(x * 64, 64), 64)
                    if y == 0:
                        gylo[line] = flat
                    if y == EDGE - 1:
                        gyhi[line] = flat
                grad_t[hx, q] = turned
        sub = total.astype(BF)
        sent = jnp.dot(spread[...], sub, preferred_element_type=F32).astype(BF)
        sending[:, pl.ds(first, 16), :] = sent.reshape(2 * SLOTS, 16, CH)
        return carry

    lax.fori_loop(0, EDGE // 2, at_hx, 0)
    for face in (gxlo, gxhi, gylo, gyhi):
        face[FACE:XMSG] = labels[...]

    subs_t = subs[...].T
    for q in range(4):
        found = jnp.dot(subs_t, acts[q], preferred_element_type=F32)
        partial[3456 + q * 256 : 3456 + (q + 1) * 256] = found.T.astype(BF)

    def at_tap(ab, carry):
        a = ab // 3
        b = lax.rem(ab, 3)
        halves = []
        for h in range(2):
            total = None
            for hx in range(4):
                for q in range(4):
                    px, py = q // 2, q % 2
                    rows = jnp.stack(
                        [
                            vol[2 * hx + px + a, 2 * hy + py + b, h : h + 4]
                            for hy in range(4)
                        ]
                    ).reshape(256, 256)
                    term = jnp.dot(grad_t[hx, q], rows, preferred_element_type=F32)
                    total = term if total is None else total + term
            halves.append(total)
        low, high = halves
        taps = [
            low[0:128, 0:128] + low[128:256, 128:256],
            low[0:128, 128:256] + high[128:256, 0:128],
            high[0:128, 0:128] + high[128:256, 128:256],
        ]
        for c in range(3):
            row = pl.multiple_of((ab * 3 + c) * CH, CH)
            partial[pl.ds(row, CH)] = taps[c].T.astype(BF)
        return carry

    lax.fori_loop(0, 9, at_tap, 0)
    partial[4480:] = jnp.zeros((SHARD * 128 - 4480, CH), BF)


def backward_kernel(
    vol_in, mask_rows, left, right, lower, upper, meta, weight, feat_grad, vol, sel, wide
):
    vol[...] = vol_in[...]
    pair_weights(
        wide, lambda a, b, c: weight[((2 - a) * 9 + (2 - b) * 3 + 2 - c) * CH :][:CH].T
    )
    fill_halo(vol, sel, meta, left, right, lower, upper)
    r = lax.broadcasted_iota(jnp.int32, (256, 256), 0)
    k = lax.broadcasted_iota(jnp.int32, (256, 256), 1)
    order = one_hot(
        (r % 2) * 128 + (r // 8 % 2) * 64 + (r // 2 % 4) * 16 + r // 16, k
    )

    def at_hx(hx, carry):
        back = conv_rows(vol, wide, 2 * hx, 2).astype(BF).reshape(2, 4, 128, 256)
        for px in range(2):
            for q in range(4):
                x = 2 * hx + px
                data = jnp.concatenate(
                    [back[px, q, :, 0:CH], back[px, q, :, CH:256]], axis=0
                )
                chosen = order * mask_rows[x, q : q + 1, :]
                out = jnp.dot(chosen, data, preferred_element_type=F32).astype(BF)
                first = pl.multiple_of(x * 64 + q * 16, 16)
                feat_grad[:, pl.ds(first, 16), :] = out.reshape(SLOTS, 16, CH)
        return carry

    lax.fori_loop(0, EDGE // 2, at_hx, 0)


VMEM_LIMIT = 56 * 1024 * 1024
VOLUME = (10, 10, 5, SLOTS, 256)


def whole(count):
    return [pl.BlockSpec(memory_space=pltpu.VMEM)] * count


def shift(value, axis, step):
    count = lax.axis_size(axis)
    if step > 0:
        pairs = [(i, i + 1) for i in range(count - 1)]
    else:
        pairs = [(i + 1, i) for i in range(count - 1)]
    return lax.ppermute(value, axis, pairs)


def exchange(xlo, xhi, ylo, yhi):
    left = shift(xhi, "gx", 1)
    right = shift(xlo, "gx", -1)
    ends = [left[FACE:XMSG], right[FACE:XMSG]]
    up = jnp.concatenate([yhi, left[FACE - 64 : FACE], right[FACE - 64 : FACE]] + ends)
    down = jnp.concatenate([ylo, left[0:64], right[0:64]] + ends)
    lower = shift(up, "gy", 1)
    upper = shift(down, "gy", -1)
    return left, right, lower, upper


def per_device(
    feats, voxel_mask, brick_coord, brick_count, route, conv_weight, down_weight, coarse_grad
):
    tiles_x = lax.axis_size("gx")
    tiles_y = lax.axis_size("gy")
    devices = tiles_x * tiles_y
    slot_ids = jnp.arange(SLOTS, dtype=jnp.int32)
    counts = brick_count[0, 0]
    occupied = jnp.where(slot_ids < BORDER, slot_ids < counts[0], slot_ids - BORDER < counts[1])
    coords = brick_coord[0, 0]
    active = (voxel_mask[0, 0] * occupied.astype(jnp.int32)[:, None]).astype(BF)
    by_chunk = active.reshape(SLOTS, EDGE, 4, 16)
    mask_rows = by_chunk.transpose(1, 2, 0, 3).reshape(EDGE, 4, 256)
    by_pair = active.reshape(SLOTS, EDGE, 4, 2, 4, 2)
    back_rows = by_pair.transpose(1, 2, 5, 3, 4, 0).reshape(EDGE, 4, 256)
    packed = 1 + coords[:, 0] + TILE * coords[:, 1] + TILE * TILE * coords[:, 2]
    labels = jnp.where(occupied, packed, 0)[:BORDER]
    labels = jnp.broadcast_to(jnp.tile(labels, 128 // BORDER)[None], (LAB, 128)).astype(BF)
    own = position_code(coords[:, 0], coords[:, 1], coords[:, 2])
    target = jnp.where(occupied, route[0, 0, :, 0] * CAP + route[0, 0, :, 1], NOWHERE)
    meta = jnp.concatenate(
        [
            jnp.broadcast_to(own[:, None], (SLOTS, 128)),
            jnp.broadcast_to(target[:, None], (SLOTS, 128)),
            jnp.tile(jnp.where(occupied, own, NOWHERE), 8)[None],
            jnp.tile(target, 8)[None],
            jnp.zeros((6, 128), jnp.int32),
        ]
    )

    params = pltpu.CompilerParams(vmem_limit_bytes=VMEM_LIMIT)
    face = jax.ShapeDtypeStruct((XMSG, CH), BF)
    volume = jax.ShapeDtypeStruct(VOLUME, BF)
    vol, mask, xlo, xhi, ylo, yhi = pl.pallas_call(
        arrange_kernel,
        out_shape=(volume, jax.ShapeDtypeStruct((8, 8, 4, SLOTS, 256), BF)) + (face,) * 4,
        in_specs=whole(3),
        out_specs=tuple(whole(6)),
        compiler_params=params,
        name="arrange",
    )(feats[0, 0], mask_rows, labels)
    around = exchange(xlo, xhi, ylo, yhi)
    returned = lax.all_to_all(
        coarse_grad[0, 0].reshape(tiles_x, CAP * 64, CH), "gx", 0, 0, tiled=True
    ).reshape(2 * SLOTS, 64, CH)

    grad_vol, gxlo, gxhi, gylo, gyhi, sending, partial = pl.pallas_call(
        forward_kernel,
        out_shape=(volume,)
        + (face,) * 4
        + (
            jax.ShapeDtypeStruct((2 * SLOTS, 64, CH), BF),
            jax.ShapeDtypeStruct((SHARD * 128, CH), BF),
        ),
        in_specs=whole(11),
        out_specs=tuple(whole(7)),
        scratch_shapes=[
            pltpu.VMEM(VOLUME, BF),
            pltpu.VMEM((320, 384), BF),
            pltpu.VMEM((18 * 256, 256), BF),
            pltpu.VMEM((4, 4, 256, 256), BF),
            pltpu.VMEM((256, 512), BF),
            pltpu.VMEM((512, 256), BF),
            pltpu.VMEM((4, 1024, 256), BF),
            pltpu.VMEM((1024, CH), BF),
        ],
        compiler_params=params,
        name="forward",
    )(vol, mask, *around, meta, conv_weight, down_weight, returned, labels)

    parts = lax.all_to_all(
        partial.reshape(devices, SHARD, CH), ("gx", "gy"), 0, 0, tiled=True
    )
    around = exchange(gxlo, gxhi, gylo, gyhi)
    feat_grad = pl.pallas_call(
        backward_kernel,
        out_shape=jax.ShapeDtypeStruct((SLOTS, VOX, CH), BF),
        in_specs=whole(8),
        out_specs=whole(1)[0],
        scratch_shapes=[
            pltpu.VMEM(VOLUME, BF),
            pltpu.VMEM((320, 384), BF),
            pltpu.VMEM((18 * 256, 256), BF),
        ],
        compiler_params=params,
        name="backward",
    )(grad_vol, back_rows, *around, meta, conv_weight)

    total = jnp.sum(parts.astype(F32), axis=0).astype(BF)
    coarse = lax.all_to_all(
        sending.reshape(tiles_x, CAP * 64, CH), "gx", 0, 0, tiled=True
    ).reshape(1, 1, 2 * SLOTS, 64, CH)
    sums = lax.all_to_all(
        jnp.broadcast_to(total[None], (devices, SHARD, CH)), ("gx", "gy"), 0, 0, tiled=True
    ).reshape(devices * SHARD, CH)
    total_slots = devices * SLOTS
    conv_grad = sums[:3456].astype(F32) * (1.0 / math.sqrt(total_slots * VOX))
    down_grad = sums[3456:4480].astype(F32) * (1.0 / math.sqrt(total_slots * VOX // 8))
    return (coarse, feat_grad[None, None], conv_grad, down_grad)


def solution(mesh):
    in_specs = (
        P("gx", "gy", None, None, None),
        P("gx", "gy", None, None),
        P("gx", "gy", None, None),
        P("gx", "gy", None),
        P("gx", "gy", None, None),
        P(),
        P(),
        P("gx", "gy", None, None, None),
    )
    out_specs = (P("gx", "gy", None, None, None), P("gx", "gy", None, None, None), P(), P())
    return jax.shard_map(
        per_device, mesh=mesh, in_specs=in_specs, out_specs=out_specs, check_vma=False
    )
```

time: 960 us -> 188 us (0.20); the launches traced: 945 us -> 187 us
  local copies, waits for them, and re-layouts: 446 us -> 12.1 us
  other arithmetic: 201 us -> 4.76 us
  waiting for transfers between devices: 148 us -> 31.9 us
  matrix products: 80.5 us -> 0 us
  Pallas kernels: 0 us -> 65.7 us
  blocking collectives: 0 us -> 31.2 us
  between operations: 16.1 us -> 0.96 us
  starting transfers between devices: 52.8 us -> 40.4 us
    psum x1 -> x0, waiting for transfers between devices: 131 us -> none  [per_device(): conv_sum, down_sum = lax.psum((conv_local, down_local), ('gx', 'gy'))]
    gather x57 -> x0, local copies, waits for them, and re-layouts: 124 us -> none  [the longest x54 105 us: padded_volume(): jnp.take(sliced, neighbour_index[:, 9 * a + 3 * b + c], axis=0)]
    slice x10 -> x0, local copies, waits for them, and re-layouts: 105 us -> none  [the longest x8 104 us: window_rows(): padded[:, a:a + EDGE, b:b + EDGE, c:c + EDGE]]
    concatenate x26 -> x0, other arithmetic: 99 us -> none  [the longest x6 26.4 us: with_halo(): jnp.concatenate([lax.ppermute(tail, axis, [(i, (i + 1) % count) for i in...]
    dot_general x86 -> x0, matrix products: 80.5 us -> none  [the longest x54 45.8 us: convolve(): jnp.dot(window_rows(padded, tap), weight[tap * CH:(tap + 1) * CH], prefer...]
    another operation x52 -> x5, local copies, waits for them, and re-layouts: 68.8 us -> 0.17 us  [the longest x2 0.08 us: per_device(): jnp.tile(jnp.where(occupied, own, NOWHERE), 8)[None]]
    pallas_call x0 -> x3, Pallas kernels: none -> 65.7 us  [the longest x1 35.5 us: per_device(): pl.pallas_call(forward_kernel, out_shape=(volume,) + (face,) * 4 + (jax.S...]
    concatenate x6 -> x3, local copies, waits for them, and re-layouts: 57.7 us -> 1.82 us  [the longest x1 1.8 us: per_device(): jnp.concatenate([jnp.broadcast_to(own[:, None], (SLOTS, 128)), jnp.broadc...]
  transfers between devices with their start and end apart: 15 -> 11, of which waited for: 5 -> 4; matrix products, arithmetic and copies ran while one was open for 12% -> 3% of each run, Pallas kernels for 0% -> 10%
where the time goes in v1:
time: 188 us; the launch traced here: 187 us
  Pallas kernels  65.7 us (35%)
  starting transfers between devices  40.4 us (21%)
  waiting for transfers between devices  31.9 us (17%)
  blocking collectives  31.2 us (17%)
  local copies, waits for them, and re-layouts  12.1 us (6%)
  other arithmetic  4.76 us (3%)
    pallas_call x1, Pallas kernels, per_device(): pl.pallas_call(forward_kernel, out_shape=(volume,) + (face,) * 4 + (jax.S...  35.5 us
    all_to_all x1, blocking collectives, per_device(): lax.all_to_all(partial.reshape(devices, SHARD, CH), ('gx', 'gy'), 0, 0, t...  31.2 us
    ppermute x8, waiting for transfers between devices, shift(): return lax.ppermute(value, axis, pairs)  25.1 us
    ppermute x8, starting transfers between devices, shift(): return lax.ppermute(value, axis, pairs)  22.1 us
    pallas_call x1, Pallas kernels, per_device(): pl.pallas_call(backward_kernel, out_shape=jax.ShapeDtypeStruct((SLOTS, VO...  18.7 us
    pallas_call x1, Pallas kernels, per_device(): pl.pallas_call(arrange_kernel, out_shape=(volume, jax.ShapeDtypeStruct((8...  11.5 us
    all_to_all x1, starting transfers between devices, per_device(): lax.all_to_all(coarse_grad[0, 0].reshape(tiles_x, CAP * 64, CH), 'gx', 0,...  8.22 us
    all_to_all x1, waiting for transfers between devices, per_device(): lax.all_to_all(sending.reshape(tiles_x, CAP * 64, CH), 'gx', 0, 0, tiled=...  6.78 us
  transfers between devices with their start and end apart: 11, of which 4 were waited for; matrix products, arithmetic and copies ran while one was open for 3% of the time, Pallas kernels for 10%

profile of v1, /device:TPU:1, one launch (start us, length us, event | category | flops | bytes accessed | tf_op | source)
XLA Modules:
  0.0 186.9 jit_solution(5425217054650117634)
XLA Ops:
  0.6 0.7 copy.24
  1.3 1.3 fusion.4
  2.6 1.3 broadcast_select_fusion
  3.9 0.8 bitcast_select_fusion
  4.8 1.0 squeeze.13
  6.0 0.8 reshape.138.mask_rows
  7.3 11.5 %arrange.1 = (bf16[10,10,5,16,256]{4,3,2,1,0:T(8,128)(2,1)}, bf16[8,8,4,16,256]{4,3,2,1,0:T(8,128)(2,1)}, bf16[528,128]{1,0:T(8,128)(2,1)}, bf16[528,128]{1,0:T(...) custom-call(bf16[16,512,128]{2,1,0:T(8,128)(2,1)} %bitcast.36, bf16[8,4,256]{2,1,0:T(4,128)(2,1)} %reshape.138.mask_rows, ...), custom_call_target="tpu_custom_call" | custom-call | tf_op jit(solution)/shard_map/arrange/pallas_call | solution.py:467
  18.8 4.4 %collective-permute-start = (bf16[528,128]{1,0:T(8,128)(2,1)}, bf16[528,128]{1,0:T(8,128)(2,1)S(1)}, u32[]{:S(2)}, u32[]{:S(2)}) collective-permute-start(bf16[528,128]{1,0:T(8,128)(2,1)} %get-tuple-element.19), channel_id=1, source_target_pairs={{0,8},{8,16},{16,24},{24,32},{32,40},{40,48},{48,56},{56,64},{64,7... | collective-permute-start | bytes 405512 | tf_op jit(solution)/shard_map/ppermute | solution.py:420
  23.2 1.3 collective-permute-start.1
  24.5 8.2 %all-to-all-start = ((bf16[16,128,128]{2,1,0:T(8,128)(2,1)}), bf16[16,128,128]{2,1,0:T(8,128)(2,1)S(1)}, u32[]{:S(2)}, u32[]{:S(2)}) async-start(bf16[16,128,128]{2,1,0:T(8,128)(2,1)} %bitcast.7), calls=%async_computation | async-start | bytes 1048576 | tf_op jit(solution)/shard_map/all_to_all | solution.py:476
  32.7 1.0 constant_dynamic-update-slice_fusion.4
  33.8 4.5 %collective-permute-start.2 = (bf16[688,128]{1,0:T(8,128)(2,1)S(1)}, bf16[688,128]{1,0:T(8,128)(2,1)S(1)}, u32[]{:S(2)}, u32[]{:S(2)}) collective-permute-start(bf16[688,128]{1,0:T(8,128)(2,1)S(1)} %get-tuple-element.42), channel_id=1, source_target_pairs={{0,1},{1,2},{2,3},{3,4},{4,5},{5,6},{6,7},{8,9},{9,10},{10,11},{11... | collective-permute-start | bytes 528392 | tf_op jit(solution)/shard_map/ppermute | solution.py:420
  38.3 1.9 %collective-permute-start.3 = (bf16[688,128]{1,0:T(8,128)(2,1)S(1)}, bf16[688,128]{1,0:T(8,128)(2,1)S(1)}, u32[]{:S(2)}, u32[]{:S(2)}) collective-permute-start(bf16[688,128]{1,0:T(8,128)(2,1)S(1)} %get-tuple-element.41), channel_id=1, source_target_pairs={{1,0},{2,1},{3,2},{4,3},{5,4},{6,5},{7,6},{9,8},{10,9},{11,10},{12... | collective-permute-start | bytes 528392 | tf_op jit(solution)/shard_map/ppermute | solution.py:420
  40.6 1.8 concatenate.17.meta
  42.4 2.7 %collective-permute-done.3.upper = bf16[688,128]{1,0:T(8,128)(2,1)S(1)} collective-permute-done((bf16[688,128]{1,0:T(8,128)(2,1)S(1)}, bf16[688,128]{1,0:T(8,128)(2,1)S(1)}, u32[]{:S(2)}, u32[]{:S(2)}) %collective-permute-start.3) | collective-permute-done | bytes 176160 | tf_op jit(solution)/shard_map/ppermute | solution.py:420
  46.0 35.5 %forward.1 = (bf16[10,10,5,16,256]{4,3,2,1,0:T(8,128)(2,1)}, bf16[528,128]{1,0:T(8,128)(2,1)}, bf16[528,128]{1,0:T(8,128)(2,1)}, bf16[528,128]{1,0:T(8,128)(2,1)...) custom-call(bf16[10,10,5,16,256]{4,3,2,1,0:T(8,128)(2,1)} %get-tuple-element.17.vol_in, ...), custom_call_target="tpu_custom_call" | custom-call | tf_op jit(solution)/shard_map/forward/pallas_call | solution.py:480
  81.5 31.2 %all_to_all.20 = bf16[128,40,128]{2,1,0:T(8,128)(2,1)S(1)} all-to-all(bf16[128,40,128]{2,1,0:T(8,128)(2,1)} %bitcast.38), channel_id=1, replica_groups=mesh['gx'=16,'gy'=8] {'gx','gy'}, dimensions={0} | all-to-all | bytes 2621440 | tf_op jit(solution)/shard_map/all_to_all | solution.py:504
  112.6 3.6 %all-to-all-start.1 = ((bf16[16,128,128]{2,1,0:T(8,128)(2,1)}), bf16[16,128,128]{2,1,0:T(8,128)(2,1)S(1)}, u32[]{:S(2)}, u32[]{:S(2)}) async-start(bf16[16,128,128]{2,1,0:T(8,128)(2,1)} %bitcast.9), calls=%async_computation.1 | async-start | bytes 1048576 | tf_op jit(solution)/shard_map/all_to_all | solution.py:523
  116.4 3.2 %collective-permute-start.4 = (bf16[528,128]{1,0:T(8,128)(2,1)S(1)}, bf16[528,128]{1,0:T(8,128)(2,1)S(1)}, u32[]{:S(2)}, u32[]{:S(2)}) collective-permute-start(bf16[528,128]{1,0:T(8,128)(2,1)S(1)} %copy-done.13), channel_id=1, source_target_pairs={{0,8},{8,16},{16,24},{24,32},{32,40},{40,48},{48,56},{56,64},{64,7... | collective-permute-start | bytes 405512 | tf_op jit(solution)/shard_map/ppermute | solution.py:420
  119.8 6.8 %all-to-all-done.1 = bf16[16,128,128]{2,1,0:T(8,128)(2,1)S(1)} async-done(((bf16[16,128,128]{2,1,0:T(8,128)(2,1)}), bf16[16,128,128]{2,1,0:T(8,128)(2,1)S(1)}, u32[]{:S(2)}, u32[]{:S(2)}) %all-to-all-start.1) | async-done | bytes 524320 | tf_op jit(solution)/shard_map/all_to_all | solution.py:523
  126.6 1.2 broadcast_in_dim.48
  127.8 6.5 %all-to-all-start.3 = ((bf16[128,40,128]{2,1,0:T(8,128)(2,1)}), bf16[128,40,128]{2,1,0:T(8,128)(2,1)S(1)}, u32[]{:S(2)}, u32[]{:S(2)}) async-start(bf16[128,40,128]{2,1,0:T(8,128)(2,1)} %broadcast_in_dim.48), calls=%async_computation.3 | async-start | bytes 2621440 | tf_op jit(solution)/shard_map/all_to_all | solution.py:526
  134.3 1.3 collective-permute-start.5
  135.7 18.7 %collective-permute-done.5.right = bf16[528,128]{1,0:T(8,128)(2,1)S(1)} collective-permute-done((bf16[528,128]{1,0:T(8,128)(2,1)S(1)}, bf16[528,128]{1,0:T(8,128)(2,1)S(1)}, u32[]{:S(2)}, u32[]{:S(2)}) %collective-permute-start.5) | collective-permute-done | bytes 135200 | tf_op jit(solution)/shard_map/ppermute | solution.py:420
  154.4 3.5 %collective-permute-start.6 = (bf16[688,128]{1,0:T(8,128)(2,1)S(1)}, bf16[688,128]{1,0:T(8,128)(2,1)S(1)}, u32[]{:S(2)}, u32[]{:S(2)}) collective-permute-start(bf16[688,128]{1,0:T(8,128)(2,1)S(1)} %get-tuple-element.34), channel_id=1, source_target_pairs={{0,1},{1,2},{2,3},{3,4},{4,5},{5,6},{6,7},{8,9},{9,10},{10,11},{11... | collective-permute-start | bytes 528392 | tf_op jit(solution)/shard_map/ppermute | solution.py:420
  157.8 2.1 %collective-permute-start.7 = (bf16[688,128]{1,0:T(8,128)(2,1)S(1)}, bf16[688,128]{1,0:T(8,128)(2,1)S(1)}, u32[]{:S(2)}, u32[]{:S(2)}) collective-permute-start(bf16[688,128]{1,0:T(8,128)(2,1)S(1)} %get-tuple-element.33), channel_id=1, source_target_pairs={{1,0},{2,1},{3,2},{4,3},{5,4},{6,5},{7,6},{9,8},{10,9},{11,10},{12... | collective-permute-start | bytes 528392 | tf_op jit(solution)/shard_map/ppermute | solution.py:420
  160.1 0.8 reshape.142.mask_rows
  160.9 3.7 %collective-permute-done.7.upper = bf16[688,128]{1,0:T(8,128)(2,1)S(1)} collective-permute-done((bf16[688,128]{1,0:T(8,128)(2,1)S(1)}, bf16[688,128]{1,0:T(8,128)(2,1)S(1)}, u32[]{:S(2)}, u32[]{:S(2)}) %collective-permute-start.7) | collective-permute-done | bytes 176160 | tf_op jit(solution)/shard_map/ppermute | solution.py:420
  165.3 18.7 %backward.1 = bf16[16,512,128]{2,1,0:T(8,128)(2,1)} custom-call(bf16[10,10,5,16,256]{4,3,2,1,0:T(8,128)(2,1)} %get-tuple-element.24.vol_in, bf16[8,4,256]{2,1,0:T(4,128)(2,1)} %reshape.142.mask_rows, bf16[528,128]{1,0:T(8,128)(2,1)} %copy-done.3, bf16[528,128]{1,0:T(8,128)(2,1)} %copy-done.4, bf16[688,128]{1,0:T(8,128)(2,1)} %copy-done.7, ...), custom_call_target="tpu_custom_call" | custom-call | tf_op jit(solution)/shard_map/backward/pallas_call | solution.py:508
  184.0 1.3 convert_multiply_fusion
  185.3 0.8 convert_multiply_fusion.1
  186.2 0.8 copy.42
  (61 shorter events, 3.3 us)
Async XLA Ops:
  18.8 14.9 %collective-permute-start = (bf16[528,128]{1,0:T(8,128)(2,1)}, bf16[528,128]{1,0:T(8,128)(2,1)S(1)}, u32[]{:S(2)}, u32[]{:S(2)}) collective-permute-start(bf16[528,128]{1,0:T(8,128)(2,1)} %get-tuple-element.19), channel_id=1, source_target_pairs={{0,8},{8,16},{16,24},{24,32},{32,40},{40,48},{48,56},{56,64},{64,7... | collective-permute-start | bytes 405512 | tf_op jit(solution)/shard_map/ppermute | solution.py:420
  23.2 10.6 %collective-permute-start.1 = (bf16[528,128]{1,0:T(8,128)(2,1)}, bf16[528,128]{1,0:T(8,128)(2,1)S(1)}, u32[]{:S(2)}, u32[]{:S(2)}) collective-permute-start(bf16[528,128]{1,0:T(8,128)(2,1)} %get-tuple-element.20), channel_id=1, source_target_pairs={{8,0},{16,8},{24,16},{32,24},{40,32},{48,40},{56,48},{64,56},{72,6... | collective-permute-start | bytes 405512 | tf_op jit(solution)/shard_map/ppermute | solution.py:420
  24.5 20.6 %all-to-all-start = ((bf16[16,128,128]{2,1,0:T(8,128)(2,1)}), bf16[16,128,128]{2,1,0:T(8,128)(2,1)S(1)}, u32[]{:S(2)}, u32[]{:S(2)}) async-start(bf16[16,128,128]{2,1,0:T(8,128)(2,1)} %bitcast.7), calls=%async_computation | async-start | bytes 1048576 | tf_op jit(solution)/shard_map/all_to_all | solution.py:476
  33.7 11.4 %copy-start.1 = (bf16[528,128]{1,0:T(8,128)(2,1)}, bf16[528,128]{1,0:T(8,128)(2,1)S(1)}, u32[]{:S(2)}) copy-start(bf16[528,128]{1,0:T(8,128)(2,1)S(1)} %collective-permute-done.left) | copy-start | bytes 405508
  33.8 11.4 %copy-start.2 = (bf16[528,128]{1,0:T(8,128)(2,1)}, bf16[528,128]{1,0:T(8,128)(2,1)S(1)}, u32[]{:S(2)}) copy-start(bf16[528,128]{1,0:T(8,128)(2,1)S(1)} %collective-permute-done.1.right) | copy-start | bytes 405508
  33.8 8.6 %collective-permute-start.2 = (bf16[688,128]{1,0:T(8,128)(2,1)S(1)}, bf16[688,128]{1,0:T(8,128)(2,1)S(1)}, u32[]{:S(2)}, u32[]{:S(2)}) collective-permute-start(bf16[688,128]{1,0:T(8,128)(2,1)S(1)} %get-tuple-element.42), channel_id=1, source_target_pairs={{0,1},{1,2},{2,3},{3,4},{4,5},{5,6},{6,7},{8,9},{9,10},{10,11},{11... | collective-permute-start | bytes 528392 | tf_op jit(solution)/shard_map/ppermute | solution.py:420
  38.3 6.8 %collective-permute-start.3 = (bf16[688,128]{1,0:T(8,128)(2,1)S(1)}, bf16[688,128]{1,0:T(8,128)(2,1)S(1)}, u32[]{:S(2)}, u32[]{:S(2)}) collective-permute-start(bf16[688,128]{1,0:T(8,128)(2,1)S(1)} %get-tuple-element.41), channel_id=1, source_target_pairs={{1,0},{2,1},{3,2},{4,3},{5,4},{6,5},{7,6},{9,8},{10,9},{11,10},{12... | collective-permute-start | bytes 528392 | tf_op jit(solution)/shard_map/ppermute | solution.py:420
  42.4 2.7 %copy-start.5 = (bf16[688,128]{1,0:T(8,128)(2,1)}, bf16[688,128]{1,0:T(8,128)(2,1)S(1)}, u32[]{:S(2)}) copy-start(bf16[688,128]{1,0:T(8,128)(2,1)S(1)} %collective-permute-done.2.lower) | copy-start | bytes 528388
  45.1 0.7 copy-start.6
  45.1 0.8 copy-start
  81.5 34.8 %copy-start.11 = (s32[1,1,16,512]{3,2,1,0:T(8,128)S(1)}, s32[1,1,16,512]{3,2,1,0:T(8,128)}, u32[]{:S(2)}) copy-start(s32[1,1,16,512]{3,2,1,0:T(8,128)} %param.9) | copy-start | bytes 98308
  81.5 34.9 %copy-start.13 = (bf16[528,128]{1,0:T(8,128)(2,1)S(1)}, bf16[528,128]{1,0:T(8,128)(2,1)}, u32[]{:S(2)}) copy-start(bf16[528,128]{1,0:T(8,128)(2,1)} %get-tuple-element.25) | copy-start | bytes 405508
  112.6 13.9 %all-to-all-start.1 = ((bf16[16,128,128]{2,1,0:T(8,128)(2,1)}), bf16[16,128,128]{2,1,0:T(8,128)(2,1)S(1)}, u32[]{:S(2)}, u32[]{:S(2)}) async-start(bf16[16,128,128]{2,1,0:T(8,128)(2,1)} %bitcast.9), calls=%async_computation.1 | async-start | bytes 1048576 | tf_op jit(solution)/shard_map/all_to_all | solution.py:523
  116.4 19.3 %collective-permute-start.4 = (bf16[528,128]{1,0:T(8,128)(2,1)S(1)}, bf16[528,128]{1,0:T(8,128)(2,1)S(1)}, u32[]{:S(2)}, u32[]{:S(2)}) collective-permute-start(bf16[528,128]{1,0:T(8,128)(2,1)S(1)} %copy-done.13), channel_id=1, source_target_pairs={{0,8},{8,16},{16,24},{24,32},{32,40},{40,48},{48,56},{56,64},{64,7... | collective-permute-start | bytes 405512 | tf_op jit(solution)/shard_map/ppermute | solution.py:420
  119.8 14.5 %copy-start.10 = (bf16[528,128]{1,0:T(8,128)(2,1)S(1)}, bf16[528,128]{1,0:T(8,128)(2,1)}, u32[]{:S(2)}) copy-start(bf16[528,128]{1,0:T(8,128)(2,1)} %get-tuple-element.27) | copy-start | bytes 405508
  127.8 6.5 %copy-start.12 = (bf16[528,128]{1,0:T(8,128)(2,1)S(1)}, bf16[528,128]{1,0:T(8,128)(2,1)}, u32[]{:S(2)}) copy-start(bf16[528,128]{1,0:T(8,128)(2,1)} %get-tuple-element.26) | copy-start | bytes 405508
  127.8 7.8 %copy-start.9 = (bf16[528,128]{1,0:T(8,128)(2,1)S(1)}, bf16[528,128]{1,0:T(8,128)(2,1)}, u32[]{:S(2)}) copy-start(bf16[528,128]{1,0:T(8,128)(2,1)} %get-tuple-element.28) | copy-start | bytes 405508
  127.8 56.2 %all-to-all-start.3 = ((bf16[128,40,128]{2,1,0:T(8,128)(2,1)}), bf16[128,40,128]{2,1,0:T(8,128)(2,1)S(1)}, u32[]{:S(2)}, u32[]{:S(2)}) async-start(bf16[128,40,128]{2,1,0:T(8,128)(2,1)} %broadcast_in_dim.48), calls=%async_computation.3 | async-start | bytes 2621440 | tf_op jit(solution)/shard_map/all_to_all | solution.py:526
  134.3 20.0 %collective-permute-start.5 = (bf16[528,128]{1,0:T(8,128)(2,1)S(1)}, bf16[528,128]{1,0:T(8,128)(2,1)S(1)}, u32[]{:S(2)}, u32[]{:S(2)}) collective-permute-start(bf16[528,128]{1,0:T(8,128)(2,1)S(1)} %copy-done.12), channel_id=1, source_target_pairs={{8,0},{16,8},{24,16},{32,24},{40,32},{48,40},{56,48},{64,56},{72,6... | collective-permute-start | bytes 405512 | tf_op jit(solution)/shard_map/ppermute | solution.py:420
  135.6 29.0 %copy-start.3 = (bf16[528,128]{1,0:T(8,128)(2,1)}, bf16[528,128]{1,0:T(8,128)(2,1)S(1)}, u32[]{:S(2)}) copy-start(bf16[528,128]{1,0:T(8,128)(2,1)S(1)} %collective-permute-done.4.left) | copy-start | bytes 405508
  154.3 10.3 %copy-start.4 = (bf16[528,128]{1,0:T(8,128)(2,1)}, bf16[528,128]{1,0:T(8,128)(2,1)S(1)}, u32[]{:S(2)}) copy-start(bf16[528,128]{1,0:T(8,128)(2,1)S(1)} %collective-permute-done.5.right) | copy-start | bytes 405508
  154.4 6.5 %collective-permute-start.6 = (bf16[688,128]{1,0:T(8,128)(2,1)S(1)}, bf16[688,128]{1,0:T(8,128)(2,1)S(1)}, u32[]{:S(2)}, u32[]{:S(2)}) collective-permute-start(bf16[688,128]{1,0:T(8,128)(2,1)S(1)} %get-tuple-element.34), channel_id=1, source_target_pairs={{0,1},{1,2},{2,3},{3,4},{4,5},{5,6},{6,7},{8,9},{9,10},{10,11},{11... | collective-permute-start | bytes 528392 | tf_op jit(solution)/shard_map/ppermute | solution.py:420
  157.8 6.8 %collective-permute-start.7 = (bf16[688,128]{1,0:T(8,128)(2,1)S(1)}, bf16[688,128]{1,0:T(8,128)(2,1)S(1)}, u32[]{:S(2)}, u32[]{:S(2)}) collective-permute-start(bf16[688,128]{1,0:T(8,128)(2,1)S(1)} %get-tuple-element.33), channel_id=1, source_target_pairs={{1,0},{2,1},{3,2},{4,3},{5,4},{6,5},{7,6},{9,8},{10,9},{11,10},{12... | collective-permute-start | bytes 528392 | tf_op jit(solution)/shard_map/ppermute | solution.py:420
  160.9 3.7 %copy-start.7 = (bf16[688,128]{1,0:T(8,128)(2,1)}, bf16[688,128]{1,0:T(8,128)(2,1)S(1)}, u32[]{:S(2)}) copy-start(bf16[688,128]{1,0:T(8,128)(2,1)S(1)} %collective-permute-done.6.lower) | copy-start | bytes 528388
  164.6 0.7 copy-start.8

commit v2 on v1

--- a/solution.py
+++ b/solution.py
@@ -58,10 +58,9 @@
     vol[xp, yp, zp // 2, :, (zp % 2) * CH : (zp % 2 + 1) * CH] = value
 
 
-def fill_halo(vol, sel, meta, left, right, lower, upper):
-    base = meta[0:SLOTS]
+def fill_halo(vol, sel, base, own, left, right, lower, upper):
     lane = lane_row()
-    own = meta[2 * SLOTS : 2 * SLOTS + 1] + VSTEP * (lane // SLOTS)
+    own = own + VSTEP * (lane // SLOTS)
     nothing = jnp.zeros((SLOTS, 128), BF)
     zs = [7, 0, 1, 2, 3, 4, 5, 6, 7, 0]
     cs = [0] + [1] * 8 + [2]
@@ -200,10 +199,87 @@
     return jnp.dot(jnp.concatenate(taps, axis=1), wide[...], preferred_element_type=F32)
 
 
-def arrange_kernel(feats, mask_rows, labels, vol, mask, xlo, xhi, ylo, yhi):
+def slot_values(coord, count, routes):
+    sub = lax.broadcasted_iota(jnp.int32, (SLOTS, 128), 0)
+    lane = lane_row()
+    base = jnp.zeros((SLOTS, 128), jnp.int32)
+    target = jnp.full((SLOTS, 128), NOWHERE, jnp.int32)
+    own = jnp.full((1, 128), NOWHERE, jnp.int32)
+    target_row = jnp.full((1, 128), NOWHERE, jnp.int32)
+    for s in range(SLOTS):
+        x, y, z = (coord[0, 0, s, d] for d in range(3))
+        live = (s if s < BORDER else s - BORDER) < count[0, 0, 0 if s < BORDER else 1]
+        code = position_code(x, y, z)
+        place = jnp.where(live, routes[0, 0, s, 0] * CAP + routes[0, 0, s, 1], NOWHERE)
+        base = jnp.where(sub == s, code, base)
+        target = jnp.where(sub == s, place, target)
+        own = jnp.where(lane % SLOTS == s, jnp.where(live, code, NOWHERE), own)
+        target_row = jnp.where(lane % SLOTS == s, place, target_row)
+    return base, target, own, target_row
+
+
+def put_labels(coord, count, faces):
+    lane = lane_row()
+    row = jnp.zeros((1, 128), jnp.int32)
+    for s in range(BORDER):
+        x, y, z = (coord[0, 0, s, d] for d in range(3))
+        label = jnp.where(s < count[0, 0, 0], 1 + x + TILE * y + TILE * TILE * z, 0)
+        row = jnp.where(lane % BORDER == s, label, row)
+    rows = jnp.broadcast_to(row.astype(F32), (LAB, 128)).astype(BF)
+    for face in faces:
+        face[FACE:XMSG] = rows
+
+
+def occupied_lanes(count, slots, lane_slot):
+    live = (lane_slot < BORDER) & (lane_slot < count[0, 0, 0])
+    live = live | ((lane_slot >= BORDER) & (lane_slot - BORDER < count[0, 0, 1]))
+    return jnp.where(live, 1.0, 0.0).astype(BF)
+
+
+def put_faces(vol, xlo, xhi, ylo, yhi):
+    r = lax.broadcasted_iota(jnp.int32, (128, 256), 0)
+    k = lax.broadcasted_iota(jnp.int32, (128, 256), 1)
+    chosen = one_hot(r // BORDER * SLOTS + r % BORDER, k)
+    for face, at, along_y in ((xlo, 1, True), (xhi, 8, True), (ylo, 1, False), (yhi, 8, False)):
+        for q in range(4):
+            tiles = []
+            for col in range(2):
+                line = 2 * q + col + 1
+                for z in range(8):
+                    place = (at, line) if along_y else (line, at)
+                    tiles.append(tile_at(vol, *place, z + 1))
+            data = jnp.concatenate(tiles, axis=0)
+            out = jnp.dot(chosen, data, preferred_element_type=F32)
+            face[q * 128 : (q + 1) * 128] = out.astype(BF)
+
+
+def faces_kernel(feats, mask_rows, coord, count, xlo, xhi, ylo, yhi):
+    r = lax.broadcasted_iota(jnp.int32, (128, 128), 0)
+    k = lax.broadcasted_iota(jnp.int32, (128, 128), 1)
+    order = one_hot((r % BORDER) * 16 + r // BORDER, k)
+    order = order * occupied_lanes(count, BORDER, lane_row() // 16)
+
+    def rows(x, q, first, last):
+        data = feats[:, x * 64 + q * 16 : x * 64 + (q + 1) * 16, :].reshape(128, CH)
+        chosen = order[first:last] * mask_rows[x, q : q + 1, 0:128]
+        return jnp.dot(chosen, data, preferred_element_type=F32).astype(BF)
+
+    for q in range(4):
+        xlo[q * 128 : (q + 1) * 128] = rows(0, q, 0, 128)
+        xhi[q * 128 : (q + 1) * 128] = rows(EDGE - 1, q, 0, 128)
+    for x in range(EDGE):
+        ylo[x * 64 : (x + 1) * 64] = rows(x, 0, 0, 64)
+        yhi[x * 64 : (x + 1) * 64] = rows(x, 3, 64, 128)
+    put_labels(coord, count, (xlo, xhi, ylo, yhi))
+
+
+def arrange(feats, mask_rows, count, vol, mask):
     r = lax.broadcasted_iota(jnp.int32, (256, 256), 0)
     k = lax.broadcasted_iota(jnp.int32, (256, 256), 1)
     order = one_hot((r % SLOTS) * 16 + r // SLOTS, k)
+    order = order * occupied_lanes(
+        count, SLOTS, lax.broadcasted_iota(jnp.int32, (1, 256), 1) // 16
+    )
     ones = jnp.ones((256, CH), BF)
 
     def at_x(x, carry):
@@ -221,48 +297,32 @@
                     mask[x, q * 2 + y, z // 2, :, (z % 2) * CH : (z % 2 + 1) * CH] = tiles[
                         y, z, :, CH : 2 * CH
                     ]
-            outer = out[:, 0:CH].reshape(2, 8, SLOTS, CH)[:, :, 0:BORDER]
-
-            @pl.when(x == 0)
-            def _():
-                xlo[q * 128 : (q + 1) * 128] = outer.reshape(128, CH).astype(BF)
-
-            @pl.when(x == EDGE - 1)
-            def _():
-                xhi[q * 128 : (q + 1) * 128] = outer.reshape(128, CH).astype(BF)
-
-            line = pl.ds(pl.multiple_of(x * 64, 64), 64)
-            if q == 0:
-                ylo[line] = outer[0].reshape(64, CH).astype(BF)
-            if q == 3:
-                yhi[line] = outer[1].reshape(64, CH).astype(BF)
         return carry
 
     lax.fori_loop(0, EDGE, at_x, 0)
-    for face in (xlo, xhi, ylo, yhi):
-        face[FACE:XMSG] = labels[...]
 
 
 def forward_kernel(
-    vol_in, mask, left, right, lower, upper, meta, weight, down, returned, labels,
-    grad_vol, gxlo, gxhi, gylo, gyhi, sending, partial,
-    vol, sel, wide, grad_t, route, spread, acts, subs,
+    feats, mask_rows, left, right, lower, upper, coord, count, routes, weight, down, returned,
+    grad_out, gxlo, gxhi, gylo, gyhi, sending, partial,
+    vol, sel, wide, grad_t, route, spread, acts, subs, mask, grad_vol, sem,
 ):
-    vol[...] = vol_in[...]
+    base, target, own, target_row = slot_values(coord, count, routes)
     pair_weights(wide, lambda a, b, c: weight[((a * 3 + b) * 3 + c) * CH :][:CH])
-    fill_halo(vol, sel, meta, left, right, lower, upper)
+    arrange(feats, mask_rows, count, vol, mask)
+    fill_halo(vol, sel, base, own, left, right, lower, upper)
 
     lane = lane_row()
     for b in range(16):
         for j in range(4):
             route[b * 16 : (b + 1) * 16, j * 128 : (j + 1) * 128] = one_hot(
-                meta[SLOTS : 2 * SLOTS] * 16 + b, lane + 128 * j
+                target * 16 + b, lane + 128 * j
             )
     block = lax.broadcasted_iota(jnp.int32, (16, 128), 0)
     for t in range(2 * SLOTS):
         for j in range(2):
             spread[t * 16 : (t + 1) * 16, j * 128 : (j + 1) * 128] = one_hot(
-                block * 64 + t, meta[2 * SLOTS + 1 : 2 * SLOTS + 2] + 64 * (lane // 16 + 8 * j)
+                block * 64 + t, target_row + 64 * (lane // 16 + 8 * j)
             )
 
     def at_hx(hx, carry):
@@ -300,30 +360,12 @@
                 )
                 grad_b = grad.astype(BF)
                 shaped = grad_b.reshape(4, 4, SLOTS, 256)
-                outer = grad.reshape(4, 4, SLOTS, 256)[:, :, 0:BORDER]
                 turned = grad_b.T
                 for hy in range(4):
                     y = 2 * hy + py
                     for p in range(4):
                         put_tile(grad_vol, x + 1, y + 1, 2 * p + 1, shaped[hy, p, :, 0:CH])
                         put_tile(grad_vol, x + 1, y + 1, 2 * p + 2, shaped[hy, p, :, CH:256])
-                    zs = jnp.stack(
-                        [outer[hy, z // 2, :, (z % 2) * CH : (z % 2 + 1) * CH] for z in range(8)]
-                    )
-                    flat = zs.reshape(64, CH).astype(BF)
-                    if px == 0:
-                        @pl.when(hx == 0)
-                        def _():
-                            gxlo[y * 64 : (y + 1) * 64] = flat
-                    else:
-                        @pl.when(hx == 3)
-                        def _():
-                            gxhi[y * 64 : (y + 1) * 64] = flat
-                    line = pl.ds(pl.multiple_of(x * 64, 64), 64)
-                    if y == 0:
-                        gylo[line] = flat
-                    if y == EDGE - 1:
-                        gyhi[line] = flat
                 grad_t[hx, q] = turned
         sub = total.astype(BF)
         sent = jnp.dot(spread[...], sub, preferred_element_type=F32).astype(BF)
@@ -331,17 +373,18 @@
         return carry
 
     lax.fori_loop(0, EDGE // 2, at_hx, 0)
-    for face in (gxlo, gxhi, gylo, gyhi):
-        face[FACE:XMSG] = labels[...]
+    copy = pltpu.make_async_copy(grad_vol, grad_out, sem)
+    copy.start()
+    put_faces(grad_vol, gxlo, gxhi, gylo, gyhi)
+    put_labels(coord, count, (gxlo, gxhi, gylo, gyhi))
 
     subs_t = subs[...].T
     for q in range(4):
         found = jnp.dot(subs_t, acts[q], preferred_element_type=F32)
         partial[3456 + q * 256 : 3456 + (q + 1) * 256] = found.T.astype(BF)
 
-    def at_tap(ab, carry):
-        a = ab // 3
-        b = lax.rem(ab, 3)
+    for ab in range(9):
+        a, b = ab // 3, ab % 3
         halves = []
         for h in range(2):
             total = None
@@ -364,26 +407,31 @@
             high[0:128, 0:128] + high[128:256, 128:256],
         ]
         for c in range(3):
-            row = pl.multiple_of((ab * 3 + c) * CH, CH)
-            partial[pl.ds(row, CH)] = taps[c].T.astype(BF)
-        return carry
-
-    lax.fori_loop(0, 9, at_tap, 0)
+            row = (ab * 3 + c) * CH
+            partial[row : row + CH] = taps[c].T.astype(BF)
     partial[4480:] = jnp.zeros((SHARD * 128 - 4480, CH), BF)
+    copy.wait()
 
 
 def backward_kernel(
-    vol_in, mask_rows, left, right, lower, upper, meta, weight, feat_grad, vol, sel, wide
+    grad_in, mask_rows, left, right, lower, upper, coord, count, routes, weight, after,
+    feat_grad, vol, sel, wide, sem,
 ):
-    vol[...] = vol_in[...]
+    copy = pltpu.make_async_copy(grad_in, vol, sem)
+    copy.start()
+    base, _, own, _ = slot_values(coord, count, routes)
     pair_weights(
         wide, lambda a, b, c: weight[((2 - a) * 9 + (2 - b) * 3 + 2 - c) * CH :][:CH].T
     )
-    fill_halo(vol, sel, meta, left, right, lower, upper)
+    copy.wait()
+    fill_halo(vol, sel, base, own, left, right, lower, upper)
     r = lax.broadcasted_iota(jnp.int32, (256, 256), 0)
     k = lax.broadcasted_iota(jnp.int32, (256, 256), 1)
     order = one_hot(
         (r % 2) * 128 + (r // 8 % 2) * 64 + (r // 2 % 4) * 16 + r // 16, k
+    )
+    order = order * occupied_lanes(
+        count, SLOTS, lax.broadcasted_iota(jnp.int32, (1, 256), 1) % SLOTS
     )
 
     def at_hx(hx, carry):
@@ -411,6 +459,14 @@
     return [pl.BlockSpec(memory_space=pltpu.VMEM)] * count
 
 
+def scalar(count):
+    return [pl.BlockSpec(memory_space=pltpu.SMEM)] * count
+
+
+def microseconds(time):
+    return pl.CostEstimate(flops=int(time * 1.1e9), bytes_accessed=1 << 20, transcendentals=0)
+
+
 def shift(value, axis, step):
     count = lax.axis_size(axis)
     if step > 0:
@@ -437,42 +493,25 @@
     tiles_x = lax.axis_size("gx")
     tiles_y = lax.axis_size("gy")
     devices = tiles_x * tiles_y
-    slot_ids = jnp.arange(SLOTS, dtype=jnp.int32)
-    counts = brick_count[0, 0]
-    occupied = jnp.where(slot_ids < BORDER, slot_ids < counts[0], slot_ids - BORDER < counts[1])
-    coords = brick_coord[0, 0]
-    active = (voxel_mask[0, 0] * occupied.astype(jnp.int32)[:, None]).astype(BF)
-    by_chunk = active.reshape(SLOTS, EDGE, 4, 16)
-    mask_rows = by_chunk.transpose(1, 2, 0, 3).reshape(EDGE, 4, 256)
+    active = voxel_mask[0, 0].astype(BF)
+    mask_rows = active.reshape(SLOTS, EDGE, 4, 16).transpose(1, 2, 0, 3).reshape(EDGE, 4, 256)
     by_pair = active.reshape(SLOTS, EDGE, 4, 2, 4, 2)
     back_rows = by_pair.transpose(1, 2, 5, 3, 4, 0).reshape(EDGE, 4, 256)
-    packed = 1 + coords[:, 0] + TILE * coords[:, 1] + TILE * TILE * coords[:, 2]
-    labels = jnp.where(occupied, packed, 0)[:BORDER]
-    labels = jnp.broadcast_to(jnp.tile(labels, 128 // BORDER)[None], (LAB, 128)).astype(BF)
-    own = position_code(coords[:, 0], coords[:, 1], coords[:, 2])
-    target = jnp.where(occupied, route[0, 0, :, 0] * CAP + route[0, 0, :, 1], NOWHERE)
-    meta = jnp.concatenate(
-        [
-            jnp.broadcast_to(own[:, None], (SLOTS, 128)),
-            jnp.broadcast_to(target[:, None], (SLOTS, 128)),
-            jnp.tile(jnp.where(occupied, own, NOWHERE), 8)[None],
-            jnp.tile(target, 8)[None],
-            jnp.zeros((6, 128), jnp.int32),
-        ]
-    )
-
-    params = pltpu.CompilerParams(vmem_limit_bytes=VMEM_LIMIT)
+    scalars = (brick_coord, brick_count, route)
+
     face = jax.ShapeDtypeStruct((XMSG, CH), BF)
     volume = jax.ShapeDtypeStruct(VOLUME, BF)
-    vol, mask, xlo, xhi, ylo, yhi = pl.pallas_call(
-        arrange_kernel,
-        out_shape=(volume, jax.ShapeDtypeStruct((8, 8, 4, SLOTS, 256), BF)) + (face,) * 4,
-        in_specs=whole(3),
-        out_specs=tuple(whole(6)),
-        compiler_params=params,
-        name="arrange",
-    )(feats[0, 0], mask_rows, labels)
-    around = exchange(xlo, xhi, ylo, yhi)
+    faces = pl.pallas_call(
+        faces_kernel,
+        grid=(1,),
+        out_shape=(face,) * 4,
+        in_specs=[pl.BlockSpec((BORDER, VOX, CH), lambda i: (0, 0, 0))] + whole(1) + scalar(2),
+        out_specs=tuple(whole(4)),
+        compiler_params=pltpu.CompilerParams(vmem_limit_bytes=VMEM_LIMIT),
+        cost_estimate=microseconds(2),
+        name="faces",
+    )(feats[0, 0], mask_rows, *scalars[:2])
+    around = exchange(*faces)
     returned = lax.all_to_all(
         coarse_grad[0, 0].reshape(tiles_x, CAP * 64, CH), "gx", 0, 0, tiled=True
     ).reshape(2 * SLOTS, 64, CH)
@@ -485,8 +524,8 @@
             jax.ShapeDtypeStruct((2 * SLOTS, 64, CH), BF),
             jax.ShapeDtypeStruct((SHARD * 128, CH), BF),
         ),
-        in_specs=whole(11),
-        out_specs=tuple(whole(7)),
+        in_specs=whole(6) + scalar(3) + whole(3),
+        out_specs=(pl.BlockSpec(memory_space=pl.ANY),) + tuple(whole(6)),
         scratch_shapes=[
             pltpu.VMEM(VOLUME, BF),
             pltpu.VMEM((320, 384), BF),
@@ -496,28 +535,38 @@
             pltpu.VMEM((512, 256), BF),
             pltpu.VMEM((4, 1024, 256), BF),
             pltpu.VMEM((1024, CH), BF),
+            pltpu.VMEM((8, 8, 4, SLOTS, 256), BF),
+            pltpu.VMEM(VOLUME, BF),
+            pltpu.SemaphoreType.DMA(()),
         ],
-        compiler_params=params,
+        compiler_params=pltpu.CompilerParams(vmem_limit_bytes=VMEM_LIMIT),
+        cost_estimate=microseconds(34),
         name="forward",
-    )(vol, mask, *around, meta, conv_weight, down_weight, returned, labels)
-
+    )(feats[0, 0], mask_rows, *around, *scalars, conv_weight, down_weight, returned)
+
+    around = exchange(gxlo, gxhi, gylo, gyhi)
     parts = lax.all_to_all(
         partial.reshape(devices, SHARD, CH), ("gx", "gy"), 0, 0, tiled=True
     )
-    around = exchange(gxlo, gxhi, gylo, gyhi)
     feat_grad = pl.pallas_call(
         backward_kernel,
         out_shape=jax.ShapeDtypeStruct((SLOTS, VOX, CH), BF),
-        in_specs=whole(8),
+        in_specs=[pl.BlockSpec(memory_space=pl.ANY)]
+        + whole(5)
+        + scalar(3)
+        + whole(1)
+        + [pl.BlockSpec(memory_space=pl.ANY)],
         out_specs=whole(1)[0],
         scratch_shapes=[
             pltpu.VMEM(VOLUME, BF),
             pltpu.VMEM((320, 384), BF),
             pltpu.VMEM((18 * 256, 256), BF),
+            pltpu.SemaphoreType.DMA(()),
         ],
-        compiler_params=params,
+        compiler_params=pltpu.CompilerParams(vmem_limit_bytes=VMEM_LIMIT),
+        cost_estimate=microseconds(18),
         name="backward",
-    )(grad_vol, back_rows, *around, meta, conv_weight)
+    )(grad_vol, back_rows, *around, *scalars, conv_weight, partial)
 
     total = jnp.sum(parts.astype(F32), axis=0).astype(BF)
     coarse = lax.all_to_all(

time: 188 us -> 147 us (0.78)
  blocking collectives: 31.2 us -> 0 us
  Pallas kernels: 65.7 us -> 54.9 us
  starting transfers between devices: 40.4 us -> 50.8 us
  waiting for transfers between devices: 31.9 us -> 27.3 us
  local copies, waits for them, and re-layouts: 12.1 us -> 9.3 us
  other arithmetic: 4.76 us -> 2.41 us
    all_to_all x1 -> x0, blocking collectives: 31.2 us -> none  [per_device(): lax.all_to_all(partial.reshape(devices, SHARD, CH), ('gx', 'gy'), 0, 0, t...]
    pallas_call x1, Pallas kernels: 11.5 us -> 2.3 us  [per_device(): pl.pallas_call(faces_kernel, grid=(1,), out_shape=(face,) * 4, in_specs=[...]
    all_to_all x0 -> x1, starting transfers between devices: none -> 8.99 us  [per_device(): lax.all_to_all(partial.reshape(devices, SHARD, CH), ('gx', 'gy'), 0, 0, t...]
    ppermute x8, waiting for transfers between devices: 25.1 us -> 19.9 us  [shift(): return lax.ppermute(value, axis, pairs)]
    all_to_all x1, waiting for transfers between devices: 6.78 us -> 3.88 us  [per_device(): lax.all_to_all(sending.reshape(tiles_x, CAP * 64, CH), 'gx', 0, 0, tiled=...]
    pallas_call x1, Pallas kernels: 35.5 us -> 33.1 us  [per_device(): pl.pallas_call(forward_kernel, out_shape=(volume,) + (face,) * 4 + (jax.S...]
    unnamed x40 -> x41, local copies, waits for them, and re-layouts: 4.19 us -> 6.34 us
    select_n x2 -> x0, other arithmetic: 2.07 us -> none  [the longest x1 1.3 us: per_device(): jnp.where(occupied, own, NOWHERE)]
  transfers between devices with their start and end apart: 11 -> 12, of which waited for: 4 -> 6; matrix products, arithmetic and copies ran while one was open for 3% -> 3% of each run, Pallas kernels for 10% -> 13%
where the time goes in v2:
time: 147 us; the launch traced here: 146 us
  Pallas kernels  54.9 us (37%)
  starting transfers between devices  50.8 us (35%)
  waiting for transfers between devices  27.3 us (19%)
  local copies, waits for them, and re-layouts  9.3 us (6%)
  other arithmetic  2.41 us (2%)
    pallas_call x1, Pallas kernels, per_device(): pl.pallas_call(forward_kernel, out_shape=(volume,) + (face,) * 4 + (jax.S...  33.1 us
    ppermute x8, starting transfers between devices, shift(): return lax.ppermute(value, axis, pairs)  22.3 us
    ppermute x8, waiting for transfers between devices, shift(): return lax.ppermute(value, axis, pairs)  19.9 us
    pallas_call x1, Pallas kernels, per_device(): pl.pallas_call(backward_kernel, out_shape=jax.ShapeDtypeStruct((SLOTS, VO...  19.5 us
    all_to_all x1, starting transfers between devices, per_device(): lax.all_to_all(partial.reshape(devices, SHARD, CH), ('gx', 'gy'), 0, 0, t...  8.99 us
    all_to_all x1, starting transfers between devices, per_device(): lax.all_to_all(coarse_grad[0, 0].reshape(tiles_x, CAP * 64, CH), 'gx', 0,...  8.22 us
    all_to_all x1, starting transfers between devices, per_device(): lax.all_to_all(jnp.broadcast_to(total[None], (devices, SHARD, CH)), ('gx'...  7.36 us
    unnamed x41, local copies, waits for them, and re-layouts  6.34 us
  transfers between devices with their start and end apart: 12, of which 6 were waited for; matrix products, arithmetic and copies ran while one was open for 3% of the time, Pallas kernels for 13%

profile of v2, /device:TPU:1, one launch (start us, length us, event | category | flops | bytes accessed | tf_op | source)
XLA Modules:
  0.0 145.7 jit_solution(16349640312480324569)
XLA Ops:
  0.6 0.9 copy.19
  1.7 0.8 reshape.36.mask_rows
  2.4 1.4 copy.21.coord
  3.8 2.3 %faces.1 = (bf16[528,128]{1,0:T(8,128)(2,1)}, bf16[528,128]{1,0:T(8,128)(2,1)}, bf16[528,128]{1,0:T(8,128)(2,1)}, bf16[528,128]{1,0:T(8,128)(2,1)}) custom-call(bf16[16,512,128]{2,1,0:T(8,128)(2,1)} %bitcast.23, bf16[8,4,256]{2,1,0:T(4,128)(2,1)} %reshape.36.mask_rows, s32[1,1,16,3]{3,2,1,0:T(8,128)} %copy.21.coord, s32[1,1,2]{2,1,0:T(1,128)} %count.5), custom_call_target="tpu_custom_call" | custom-call | flops 2200000000 | bytes 1048576 | tf_op jit(solution)/shard_map/faces/pallas_call | solution.py:504
  6.1 4.5 %collective-permute-start = (bf16[528,128]{1,0:T(8,128)(2,1)}, bf16[528,128]{1,0:T(8,128)(2,1)S(1)}, u32[]{:S(2)}, u32[]{:S(2)}) collective-permute-start(bf16[528,128]{1,0:T(8,128)(2,1)} %get-tuple-element.15), channel_id=1, source_target_pairs={{0,8},{8,16},{16,24},{24,32},{32,40},{40,48},{48,56},{56,64},{64,7... | collective-permute-start | bytes 405512 | tf_op jit(solution)/shard_map/ppermute | solution.py:476
  10.6 1.3 collective-permute-start.1
  11.9 8.2 %all-to-all-start = ((bf16[16,128,128]{2,1,0:T(8,128)(2,1)}), bf16[16,128,128]{2,1,0:T(8,128)(2,1)S(1)}, u32[]{:S(2)}, u32[]{:S(2)}) async-start(bf16[16,128,128]{2,1,0:T(8,128)(2,1)} %bitcast.3), calls=%async_computation | async-start | bytes 1048576 | tf_op jit(solution)/shard_map/all_to_all | solution.py:515
  20.1 1.0 constant_dynamic-update-slice_fusion.4
  21.2 4.5 %collective-permute-start.2 = (bf16[688,128]{1,0:T(8,128)(2,1)S(1)}, bf16[688,128]{1,0:T(8,128)(2,1)S(1)}, u32[]{:S(2)}, u32[]{:S(2)}) collective-permute-start(bf16[688,128]{1,0:T(8,128)(2,1)S(1)} %get-tuple-element.35), channel_id=1, source_target_pairs={{0,1},{1,2},{2,3},{3,4},{4,5},{5,6},{6,7},{8,9},{9,10},{10,11},{11... | collective-permute-start | bytes 528392 | tf_op jit(solution)/shard_map/ppermute | solution.py:476
  25.7 1.9 %collective-permute-start.3 = (bf16[688,128]{1,0:T(8,128)(2,1)S(1)}, bf16[688,128]{1,0:T(8,128)(2,1)S(1)}, u32[]{:S(2)}, u32[]{:S(2)}) collective-permute-start(bf16[688,128]{1,0:T(8,128)(2,1)S(1)} %get-tuple-element.34), channel_id=1, source_target_pairs={{1,0},{2,1},{3,2},{4,3},{5,4},{6,5},{7,6},{9,8},{10,9},{11,10},{12... | collective-permute-start | bytes 528392 | tf_op jit(solution)/shard_map/ppermute | solution.py:476
  27.7 0.7 copy.23.routes
  28.4 4.1 %collective-permute-done.3.upper = bf16[688,128]{1,0:T(8,128)(2,1)S(1)} collective-permute-done((bf16[688,128]{1,0:T(8,128)(2,1)S(1)}, bf16[688,128]{1,0:T(8,128)(2,1)S(1)}, u32[]{:S(2)}, u32[]{:S(2)}) %collective-permute-start.3) | collective-permute-done | bytes 176160 | tf_op jit(solution)/shard_map/ppermute | solution.py:476
  33.4 33.1 %forward.1 = (bf16[10,10,5,16,256]{4,3,2,1,0:T(8,128)(2,1)}, bf16[528,128]{1,0:T(8,128)(2,1)}, bf16[528,128]{1,0:T(8,128)(2,1)}, bf16[528,128]{1,0:T(8,128)(2,1)...) custom-call(bf16[16,512,128]{2,1,0:T(8,128)(2,1)} %bitcast.24, ...), custom_call_target="tpu_custom_call" | custom-call | flops 37399998464 | bytes 1048576 | tf_op jit(solution)/shard_map/forward/pallas_call | solution.py:519
  66.5 9.0 %all-to-all-start.2 = ((bf16[128,40,128]{2,1,0:T(8,128)(2,1)}), bf16[128,40,128]{2,1,0:T(8,128)(2,1)S(1)}, u32[]{:S(2)}, u32[]{:S(2)}) async-start(bf16[128,40,128]{2,1,0:T(8,128)(2,1)} %bitcast.18), calls=%async_computation.2 | async-start | bytes 2621440 | tf_op jit(solution)/shard_map/all_to_all | solution.py:548
  75.6 3.4 %collective-permute-start.4 = (bf16[528,128]{1,0:T(8,128)(2,1)S(1)}, bf16[528,128]{1,0:T(8,128)(2,1)S(1)}, u32[]{:S(2)}, u32[]{:S(2)}) collective-permute-start(bf16[528,128]{1,0:T(8,128)(2,1)S(1)} %copy-done.13), channel_id=1, source_target_pairs={{0,8},{8,16},{16,24},{24,32},{32,40},{40,48},{48,56},{56,64},{64,7... | collective-permute-start | bytes 405512 | tf_op jit(solution)/shard_map/ppermute | solution.py:476
  79.0 1.3 collective-permute-start.5
  80.3 13.0 %collective-permute-done.4.left = bf16[528,128]{1,0:T(8,128)(2,1)S(1)} collective-permute-done((bf16[528,128]{1,0:T(8,128)(2,1)S(1)}, bf16[528,128]{1,0:T(8,128)(2,1)S(1)}, u32[]{:S(2)}, u32[]{:S(2)}) %collective-permute-start.4) | collective-permute-done | bytes 135200 | tf_op jit(solution)/shard_map/ppermute | solution.py:476
  93.4 2.7 %collective-permute-done.5.right = bf16[528,128]{1,0:T(8,128)(2,1)S(1)} collective-permute-done((bf16[528,128]{1,0:T(8,128)(2,1)S(1)}, bf16[528,128]{1,0:T(8,128)(2,1)S(1)}, u32[]{:S(2)}, u32[]{:S(2)}) %collective-permute-start.5) | collective-permute-done | bytes 135200 | tf_op jit(solution)/shard_map/ppermute | solution.py:476
  96.1 1.6 %all-to-all-done.2 = bf16[128,40,128]{2,1,0:T(8,128)(2,1)S(1)} async-done(((bf16[128,40,128]{2,1,0:T(8,128)(2,1)}), bf16[128,40,128]{2,1,0:T(8,128)(2,1)S(1)}, u32[]{:S(2)}, u32[]{:S(2)}) %all-to-all-start.2) | async-done | bytes 1310752 | tf_op jit(solution)/shard_map/all_to_all | solution.py:548
  97.7 3.9 %all-to-all-start.1 = ((bf16[16,128,128]{2,1,0:T(8,128)(2,1)}), bf16[16,128,128]{2,1,0:T(8,128)(2,1)S(1)}, u32[]{:S(2)}, u32[]{:S(2)}) async-start(bf16[16,128,128]{2,1,0:T(8,128)(2,1)} %bitcast.5), calls=%async_computation.1 | async-start | bytes 1048576 | tf_op jit(solution)/shard_map/all_to_all | solution.py:572
  101.6 3.5 %collective-permute-start.6 = (bf16[688,128]{1,0:T(8,128)(2,1)S(1)}, bf16[688,128]{1,0:T(8,128)(2,1)S(1)}, u32[]{:S(2)}, u32[]{:S(2)}) collective-permute-start(bf16[688,128]{1,0:T(8,128)(2,1)S(1)} %get-tuple-element.27), channel_id=1, source_target_pairs={{0,1},{1,2},{2,3},{3,4},{4,5},{5,6},{6,7},{8,9},{9,10},{10,11},{11... | collective-permute-start | bytes 528392 | tf_op jit(solution)/shard_map/ppermute | solution.py:476
  105.1 1.9 %collective-permute-start.7 = (bf16[688,128]{1,0:T(8,128)(2,1)S(1)}, bf16[688,128]{1,0:T(8,128)(2,1)S(1)}, u32[]{:S(2)}, u32[]{:S(2)}) collective-permute-start(bf16[688,128]{1,0:T(8,128)(2,1)S(1)} %get-tuple-element.26), channel_id=1, source_target_pairs={{1,0},{2,1},{3,2},{4,3},{5,4},{6,5},{7,6},{9,8},{10,9},{11,10},{12... | collective-permute-start | bytes 528392 | tf_op jit(solution)/shard_map/ppermute | solution.py:476
  107.1 0.8 reshape.40.mask_rows
  108.1 3.9 %all-to-all-done.1 = bf16[16,128,128]{2,1,0:T(8,128)(2,1)S(1)} async-done(((bf16[16,128,128]{2,1,0:T(8,128)(2,1)}), bf16[16,128,128]{2,1,0:T(8,128)(2,1)S(1)}, u32[]{:S(2)}, u32[]{:S(2)}) %all-to-all-start.1) | async-done | bytes 524320 | tf_op jit(solution)/shard_map/all_to_all | solution.py:572
  111.9 1.3 broadcast_in_dim.10
  113.2 7.4 %all-to-all-start.3 = ((bf16[128,40,128]{2,1,0:T(8,128)(2,1)}), bf16[128,40,128]{2,1,0:T(8,128)(2,1)S(1)}, u32[]{:S(2)}, u32[]{:S(2)}) async-start(bf16[128,40,128]{2,1,0:T(8,128)(2,1)} %broadcast_in_dim.10), calls=%async_computation.3 | async-start | bytes 2621440 | tf_op jit(solution)/shard_map/all_to_all | solution.py:575
  120.6 0.6 copy-done.8
  121.3 19.5 %backward.1 = bf16[16,512,128]{2,1,0:T(8,128)(2,1)} custom-call(bf16[10,10,5,16,256]{4,3,2,1,0:T(8,128)(2,1)} %get-tuple-element.20.grad_in, bf16[8,4,256]{2,1,0:T(4,128)(2,1)} %reshape.40.mask_rows, bf16[528,128]{1,0:T(8,128)(2,1)} %copy-done.3, bf16[528,128]{1,0:T(8,128)(2,1)} %copy-done.4, bf16[688,128]{1,0:T(8,128)(2,1)} %copy-done.8, ...), custom_call_target="tpu_custom_call" | custom-call | flops 19800000512 | bytes 1048576 | tf_op jit(solution)/shard_map/backward/pallas_call | solution.py:551
  140.8 1.9 %all-to-all-done.3 = bf16[128,40,128]{2,1,0:T(8,128)(2,1)S(1)} async-done(((bf16[128,40,128]{2,1,0:T(8,128)(2,1)}), bf16[128,40,128]{2,1,0:T(8,128)(2,1)S(1)}, u32[]{:S(2)}, u32[]{:S(2)}) %all-to-all-start.3) | async-done | bytes 1310752 | tf_op jit(solution)/shard_map/all_to_all | solution.py:575
  142.7 1.3 convert_multiply_fusion
  144.1 0.8 convert_multiply_fusion.1
  144.9 0.8 copy.44
  (47 shorter events, 1.5 us)
Async XLA Ops:
  6.1 21.6 %copy-start.7 = (s32[1,1,16,2]{2,3,1,0:T(2,128)S(1)}, s32[1,1,16,2]{2,3,1,0:T(2,128)}, u32[]{:S(2)}) copy-start(s32[1,1,16,2]{2,3,1,0:T(2,128)} %param.12) | copy-start | bytes 388
  6.1 15.0 %collective-permute-start = (bf16[528,128]{1,0:T(8,128)(2,1)}, bf16[528,128]{1,0:T(8,128)(2,1)S(1)}, u32[]{:S(2)}, u32[]{:S(2)}) collective-permute-start(bf16[528,128]{1,0:T(8,128)(2,1)} %get-tuple-element.15), channel_id=1, source_target_pairs={{0,8},{8,16},{16,24},{24,32},{32,40},{40,48},{48,56},{56,64},{64,7... | collective-permute-start | bytes 405512 | tf_op jit(solution)/shard_map/ppermute | solution.py:476
  10.6 10.6 %collective-permute-start.1 = (bf16[528,128]{1,0:T(8,128)(2,1)}, bf16[528,128]{1,0:T(8,128)(2,1)S(1)}, u32[]{:S(2)}, u32[]{:S(2)}) collective-permute-start(bf16[528,128]{1,0:T(8,128)(2,1)} %get-tuple-element.16), channel_id=1, source_target_pairs={{8,0},{16,8},{24,16},{32,24},{40,32},{48,40},{56,48},{64,56},{72,6... | collective-permute-start | bytes 405512 | tf_op jit(solution)/shard_map/ppermute | solution.py:476
  11.9 20.6 %all-to-all-start = ((bf16[16,128,128]{2,1,0:T(8,128)(2,1)}), bf16[16,128,128]{2,1,0:T(8,128)(2,1)S(1)}, u32[]{:S(2)}, u32[]{:S(2)}) async-start(bf16[16,128,128]{2,1,0:T(8,128)(2,1)} %bitcast.3), calls=%async_computation | async-start | bytes 1048576 | tf_op jit(solution)/shard_map/all_to_all | solution.py:515
  21.1 11.4 %copy-start.5 = (bf16[528,128]{1,0:T(8,128)(2,1)}, bf16[528,128]{1,0:T(8,128)(2,1)S(1)}, u32[]{:S(2)}) copy-start(bf16[528,128]{1,0:T(8,128)(2,1)S(1)} %collective-permute-done.left) | copy-start | bytes 405508
  21.2 11.4 %copy-start.6 = (bf16[528,128]{1,0:T(8,128)(2,1)}, bf16[528,128]{1,0:T(8,128)(2,1)S(1)}, u32[]{:S(2)}) copy-start(bf16[528,128]{1,0:T(8,128)(2,1)S(1)} %collective-permute-done.1.right) | copy-start | bytes 405508
  21.2 7.1 %collective-permute-start.2 = (bf16[688,128]{1,0:T(8,128)(2,1)S(1)}, bf16[688,128]{1,0:T(8,128)(2,1)S(1)}, u32[]{:S(2)}, u32[]{:S(2)}) collective-permute-start(bf16[688,128]{1,0:T(8,128)(2,1)S(1)} %get-tuple-element.35), channel_id=1, source_target_pairs={{0,1},{1,2},{2,3},{3,4},{4,5},{5,6},{6,7},{8,9},{9,10},{10,11},{11... | collective-permute-start | bytes 528392 | tf_op jit(solution)/shard_map/ppermute | solution.py:476
  25.7 6.8 %collective-permute-start.3 = (bf16[688,128]{1,0:T(8,128)(2,1)S(1)}, bf16[688,128]{1,0:T(8,128)(2,1)S(1)}, u32[]{:S(2)}, u32[]{:S(2)}) collective-permute-start(bf16[688,128]{1,0:T(8,128)(2,1)S(1)} %get-tuple-element.34), channel_id=1, source_target_pairs={{1,0},{2,1},{3,2},{4,3},{5,4},{6,5},{7,6},{9,8},{10,9},{11,10},{12... | collective-permute-start | bytes 528392 | tf_op jit(solution)/shard_map/ppermute | solution.py:476
  28.4 4.2 %copy-start.10 = (bf16[688,128]{1,0:T(8,128)(2,1)}, bf16[688,128]{1,0:T(8,128)(2,1)S(1)}, u32[]{:S(2)}) copy-start(bf16[688,128]{1,0:T(8,128)(2,1)S(1)} %collective-permute-done.2.lower) | copy-start | bytes 528388
  32.5 0.7 copy-start.11
  32.5 0.8 copy-start
  66.5 9.0 %copy-start.13 = (bf16[528,128]{1,0:T(8,128)(2,1)S(1)}, bf16[528,128]{1,0:T(8,128)(2,1)}, u32[]{:S(2)}) copy-start(bf16[528,128]{1,0:T(8,128)(2,1)} %get-tuple-element.21) | copy-start | bytes 405508
  66.5 12.5 %copy-start.12 = (bf16[528,128]{1,0:T(8,128)(2,1)S(1)}, bf16[528,128]{1,0:T(8,128)(2,1)}, u32[]{:S(2)}) copy-start(bf16[528,128]{1,0:T(8,128)(2,1)} %get-tuple-element.22) | copy-start | bytes 405508
  66.5 13.8 %copy-start.2 = (bf16[528,128]{1,0:T(8,128)(2,1)S(1)}, bf16[528,128]{1,0:T(8,128)(2,1)}, u32[]{:S(2)}) copy-start(bf16[528,128]{1,0:T(8,128)(2,1)} %get-tuple-element.24) | copy-start | bytes 405508
  66.5 13.8 %copy-start.1 = (bf16[528,128]{1,0:T(8,128)(2,1)S(1)}, bf16[528,128]{1,0:T(8,128)(2,1)}, u32[]{:S(2)}) copy-start(bf16[528,128]{1,0:T(8,128)(2,1)} %get-tuple-element.23) | copy-start | bytes 405508
  66.5 31.2 %all-to-all-start.2 = ((bf16[128,40,128]{2,1,0:T(8,128)(2,1)}), bf16[128,40,128]{2,1,0:T(8,128)(2,1)S(1)}, u32[]{:S(2)}, u32[]{:S(2)}) async-start(bf16[128,40,128]{2,1,0:T(8,128)(2,1)} %bitcast.18), calls=%async_computation.2 | async-start | bytes 2621440 | tf_op jit(solution)/shard_map/all_to_all | solution.py:548
  75.6 17.8 %collective-permute-start.4 = (bf16[528,128]{1,0:T(8,128)(2,1)S(1)}, bf16[528,128]{1,0:T(8,128)(2,1)S(1)}, u32[]{:S(2)}, u32[]{:S(2)}) collective-permute-start(bf16[528,128]{1,0:T(8,128)(2,1)S(1)} %copy-done.13), channel_id=1, source_target_pairs={{0,8},{8,16},{16,24},{24,32},{32,40},{40,48},{48,56},{56,64},{64,7... | collective-permute-start | bytes 405512 | tf_op jit(solution)/shard_map/ppermute | solution.py:476
  79.0 17.1 %collective-permute-start.5 = (bf16[528,128]{1,0:T(8,128)(2,1)S(1)}, bf16[528,128]{1,0:T(8,128)(2,1)S(1)}, u32[]{:S(2)}, u32[]{:S(2)}) collective-permute-start(bf16[528,128]{1,0:T(8,128)(2,1)S(1)} %copy-done.12), channel_id=1, source_target_pairs={{8,0},{16,8},{24,16},{32,24},{40,32},{48,40},{56,48},{64,56},{72,6... | collective-permute-start | bytes 405512 | tf_op jit(solution)/shard_map/ppermute | solution.py:476
  93.3 19.9 %copy-start.3 = (bf16[528,128]{1,0:T(8,128)(2,1)}, bf16[528,128]{1,0:T(8,128)(2,1)S(1)}, u32[]{:S(2)}) copy-start(bf16[528,128]{1,0:T(8,128)(2,1)S(1)} %collective-permute-done.4.left) | copy-start | bytes 405508
  96.1 17.1 %copy-start.4 = (bf16[528,128]{1,0:T(8,128)(2,1)}, bf16[528,128]{1,0:T(8,128)(2,1)S(1)}, u32[]{:S(2)}) copy-start(bf16[528,128]{1,0:T(8,128)(2,1)S(1)} %collective-permute-done.5.right) | copy-start | bytes 405508
  97.7 14.2 %all-to-all-start.1 = ((bf16[16,128,128]{2,1,0:T(8,128)(2,1)}), bf16[16,128,128]{2,1,0:T(8,128)(2,1)S(1)}, u32[]{:S(2)}, u32[]{:S(2)}) async-start(bf16[16,128,128]{2,1,0:T(8,128)(2,1)} %bitcast.5), calls=%async_computation.1 | async-start | bytes 1048576 | tf_op jit(solution)/shard_map/all_to_all | solution.py:572
  101.6 19.0 %collective-permute-start.6 = (bf16[688,128]{1,0:T(8,128)(2,1)S(1)}, bf16[688,128]{1,0:T(8,128)(2,1)S(1)}, u32[]{:S(2)}, u32[]{:S(2)}) collective-permute-start(bf16[688,128]{1,0:T(8,128)(2,1)S(1)} %get-tuple-element.27), channel_id=1, source_target_pairs={{0,1},{1,2},{2,3},{3,4},{4,5},{5,6},{6,7},{8,9},{9,10},{10,11},{11... | collective-permute-start | bytes 528392 | tf_op jit(solution)/shard_map/ppermute | solution.py:476
  105.1 15.5 %collective-permute-start.7 = (bf16[688,128]{1,0:T(8,128)(2,1)S(1)}, bf16[688,128]{1,0:T(8,128)(2,1)S(1)}, u32[]{:S(2)}, u32[]{:S(2)}) collective-permute-start(bf16[688,128]{1,0:T(8,128)(2,1)S(1)} %get-tuple-element.26), channel_id=1, source_target_pairs={{1,0},{2,1},{3,2},{4,3},{5,4},{6,5},{7,6},{9,8},{10,9},{11,10},{12... | collective-permute-start | bytes 528392 | tf_op jit(solution)/shard_map/ppermute | solution.py:476
  113.2 29.5 %all-to-all-start.3 = ((bf16[128,40,128]{2,1,0:T(8,128)(2,1)}), bf16[128,40,128]{2,1,0:T(8,128)(2,1)S(1)}, u32[]{:S(2)}, u32[]{:S(2)}) async-start(bf16[128,40,128]{2,1,0:T(8,128)(2,1)} %broadcast_in_dim.10), calls=%async_computation.3 | async-start | bytes 2621440 | tf_op jit(solution)/shard_map/all_to_all | solution.py:575
  120.6 0.7 copy-start.8
  120.6 0.7 copy-start.9

commit v3 on v2

--- a/solution.py
+++ b/solution.py
@@ -414,7 +414,7 @@
 
 
 def backward_kernel(
-    grad_in, mask_rows, left, right, lower, upper, coord, count, routes, weight, after,
+    grad_in, mask_rows, left, right, lower, upper, coord, count, routes, weight,
     feat_grad, vol, sel, wide, sem,
 ):
     copy = pltpu.make_async_copy(grad_in, vol, sem)
@@ -451,6 +451,10 @@
     lax.fori_loop(0, EDGE // 2, at_hx, 0)
 
 
+def later_kernel(value, after, same):
+    same[...] = value[...]
+
+
 VMEM_LIMIT = 56 * 1024 * 1024
 VOLUME = (10, 10, 5, SLOTS, 256)
 
@@ -512,8 +516,17 @@
         name="faces",
     )(feats[0, 0], mask_rows, *scalars[:2])
     around = exchange(*faces)
+    cotangents = pl.pallas_call(
+        later_kernel,
+        out_shape=jax.ShapeDtypeStruct((tiles_x, CAP * 64, CH), BF),
+        in_specs=whole(1) + [pl.BlockSpec(memory_space=pl.ANY)],
+        out_specs=whole(1)[0],
+        compiler_params=pltpu.CompilerParams(vmem_limit_bytes=VMEM_LIMIT),
+        cost_estimate=microseconds(1),
+        name="later",
+    )(coarse_grad[0, 0].reshape(tiles_x, CAP * 64, CH), around[0])
     returned = lax.all_to_all(
-        coarse_grad[0, 0].reshape(tiles_x, CAP * 64, CH), "gx", 0, 0, tiled=True
+        cotangents, "gx", 0, 0, tiled=True
     ).reshape(2 * SLOTS, 64, CH)
 
     grad_vol, gxlo, gxhi, gylo, gyhi, sending, partial = pl.pallas_call(
@@ -545,17 +558,15 @@
     )(feats[0, 0], mask_rows, *around, *scalars, conv_weight, down_weight, returned)
 
     around = exchange(gxlo, gxhi, gylo, gyhi)
-    parts = lax.all_to_all(
-        partial.reshape(devices, SHARD, CH), ("gx", "gy"), 0, 0, tiled=True
-    )
+    shares = tiles_x * SHARD
+    parts = lax.all_to_all(partial.reshape(tiles_y, shares, CH), "gy", 0, 0, tiled=True)
     feat_grad = pl.pallas_call(
         backward_kernel,
         out_shape=jax.ShapeDtypeStruct((SLOTS, VOX, CH), BF),
         in_specs=[pl.BlockSpec(memory_space=pl.ANY)]
         + whole(5)
         + scalar(3)
-        + whole(1)
-        + [pl.BlockSpec(memory_space=pl.ANY)],
+        + whole(1),
         out_specs=whole(1)[0],
         scratch_shapes=[
             pltpu.VMEM(VOLUME, BF),
@@ -566,14 +577,15 @@
         compiler_params=pltpu.CompilerParams(vmem_limit_bytes=VMEM_LIMIT),
         cost_estimate=microseconds(18),
         name="backward",
-    )(grad_vol, back_rows, *around, *scalars, conv_weight, partial)
-
-    total = jnp.sum(parts.astype(F32), axis=0).astype(BF)
-    coarse = lax.all_to_all(
-        sending.reshape(tiles_x, CAP * 64, CH), "gx", 0, 0, tiled=True
-    ).reshape(1, 1, 2 * SLOTS, 64, CH)
+    )(grad_vol, back_rows, *around, *scalars, conv_weight)
+
+    total = jnp.sum(parts.astype(F32), axis=0).astype(BF).reshape(tiles_x, SHARD, CH)
+    message = jnp.concatenate([sending.reshape(tiles_x, CAP * 64, CH), total], axis=1)
+    parts = lax.all_to_all(message, "gx", 0, 0, tiled=True)
+    coarse = parts[:, : CAP * 64].reshape(1, 1, 2 * SLOTS, 64, CH)
+    total = jnp.sum(parts[:, CAP * 64 :].astype(F32), axis=0).astype(BF)
     sums = lax.all_to_all(
-        jnp.broadcast_to(total[None], (devices, SHARD, CH)), ("gx", "gy"), 0, 0, tiled=True
+        jnp.broadcast_to(total[None], (devices, SHARD, CH)), ("gy", "gx"), 0, 0, tiled=True
     ).reshape(devices * SHARD, CH)
     total_slots = devices * SLOTS
     conv_grad = sums[:3456].astype(F32) * (1.0 / math.sqrt(total_slots * VOX))

time: 147 us -> 144 us (0.980)
  waiting for transfers between devices: 27.3 us -> 20.9 us
  local copies, waits for them, and re-layouts: 9.3 us -> 11.4 us
  Pallas kernels: 54.9 us -> 56.8 us
    ppermute x8, waiting for transfers between devices: 19.9 us -> 3.55 us  [shift(): return lax.ppermute(value, axis, pairs)]
    all_to_all x4, waiting for transfers between devices: 7.44 us -> 17.4 us  [the longest x1 11.6 us: per_device(): lax.all_to_all(partial.reshape(tiles_y, shares, CH), 'gy', 0, 0, tiled=True)]
    pallas_call x0 -> x1, Pallas kernels: none -> 1.88 us  [per_device(): pl.pallas_call(later_kernel, out_shape=jax.ShapeDtypeStruct((tiles_x, CAP...]
    all_to_all x4, starting transfers between devices: 28.5 us -> 26.8 us  [the longest x1 8.23 us: per_device(): lax.all_to_all(cotangents, 'gx', 0, 0, tiled=True)]
    unnamed x41 -> x42, local copies, waits for them, and re-layouts: 6.34 us -> 7.65 us
  transfers between devices with their start and end apart: 12 -> 12, of which waited for: 6 -> 7; matrix products, arithmetic and copies ran while one was open for 3% -> 5% of each run, Pallas kernels for 13% -> 15%
where the time goes in v3:
time: 144 us; the launch traced here: 143 us
  Pallas kernels  56.8 us (39%)
  starting transfers between devices  49.4 us (34%)
  waiting for transfers between devices  20.9 us (15%)
  local copies, waits for them, and re-layouts  11.4 us (8%)
  other arithmetic  3.31 us (2%)
    pallas_call x1, Pallas kernels, per_device(): pl.pallas_call(forward_kernel, out_shape=(volume,) + (face,) * 4 + (jax.S...  33.1 us
    ppermute x8, starting transfers between devices, shift(): return lax.ppermute(value, axis, pairs)  22.6 us
    pallas_call x1, Pallas kernels, per_device(): pl.pallas_call(backward_kernel, out_shape=jax.ShapeDtypeStruct((SLOTS, VO...  19.5 us
    all_to_all x1, waiting for transfers between devices, per_device(): lax.all_to_all(partial.reshape(tiles_y, shares, CH), 'gy', 0, 0, tiled=True)  11.6 us
    all_to_all x1, starting transfers between devices, per_device(): lax.all_to_all(cotangents, 'gx', 0, 0, tiled=True)  8.23 us
    unnamed x42, local copies, waits for them, and re-layouts  7.65 us
    all_to_all x1, starting transfers between devices, per_device(): parts = lax.all_to_all(message, 'gx', 0, 0, tiled=True)  6.56 us
    all_to_all x1, starting transfers between devices, per_device(): lax.all_to_all(partial.reshape(tiles_y, shares, CH), 'gy', 0, 0, tiled=True)  6.2 us
  transfers between devices with their start and end apart: 12, of which 7 were waited for; matrix products, arithmetic and copies ran while one was open for 5% of the time, Pallas kernels for 15%

profile of v3, /device:TPU:1, one launch (start us, length us, event | category | flops | bytes accessed | tf_op | source)
XLA Modules:
  0.0 142.8 jit_solution(7678094686418966914)
XLA Ops:
  0.6 1.4 copy.21.coord
  2.0 0.9 copy.19
  3.0 0.8 reshape.39.mask_rows
  3.8 2.3 %faces.1 = (bf16[528,128]{1,0:T(8,128)(2,1)}, bf16[528,128]{1,0:T(8,128)(2,1)}, bf16[528,128]{1,0:T(8,128)(2,1)}, bf16[528,128]{1,0:T(8,128)(2,1)}) custom-call(bf16[16,512,128]{2,1,0:T(8,128)(2,1)} %bitcast.26, bf16[8,4,256]{2,1,0:T(4,128)(2,1)} %reshape.39.mask_rows, s32[1,1,16,3]{3,2,1,0:T(8,128)} %copy.21.coord, s32[1,1,2]{2,1,0:T(1,128)} %count.5), custom_call_target="tpu_custom_call" | custom-call | flops 2200000000 | bytes 1048576 | tf_op jit(solution)/shard_map/faces/pallas_call | solution.py:508
  6.1 4.4 %collective-permute-start = (bf16[528,128]{1,0:T(8,128)(2,1)}, bf16[528,128]{1,0:T(8,128)(2,1)S(1)}, u32[]{:S(2)}, u32[]{:S(2)}) collective-permute-start(bf16[528,128]{1,0:T(8,128)(2,1)} %get-tuple-element.15), channel_id=1, source_target_pairs={{0,8},{8,16},{16,24},{24,32},{32,40},{40,48},{48,56},{56,64},{64,7... | collective-permute-start | bytes 405512 | tf_op jit(solution)/shard_map/ppermute | solution.py:480
  10.5 1.3 collective-permute-start.1
  11.8 1.0 constant_dynamic-update-slice_fusion.4
  13.7 1.9 %later.1 = bf16[16,128,128]{2,1,0:T(8,128)(2,1)} custom-call(bf16[16,128,128]{2,1,0:T(8,128)(2,1)} %bitcast.28, bf16[528,128]{1,0:T(8,128)(2,1)} %copy-done.6), custom_call_target="tpu_custom_call" | custom-call | flops 1100000000 | bytes 1048576 | tf_op jit(solution)/shard_map/later/pallas_call | solution.py:519
  15.5 8.2 %all-to-all-start = ((bf16[16,128,128]{2,1,0:T(8,128)(2,1)}), bf16[16,128,128]{2,1,0:T(8,128)(2,1)S(1)}, u32[]{:S(2)}, u32[]{:S(2)}) async-start(bf16[16,128,128]{2,1,0:T(8,128)(2,1)} %later.1), calls=%async_computation | async-start | bytes 1048576 | tf_op jit(solution)/shard_map/all_to_all | solution.py:528
  23.8 0.7 constant_dynamic-update-slice_fusion.8
  25.3 3.7 %collective-permute-start.3 = (bf16[688,128]{1,0:T(8,128)(2,1)S(1)}, bf16[688,128]{1,0:T(8,128)(2,1)S(1)}, u32[]{:S(2)}, u32[]{:S(2)}) collective-permute-start(bf16[688,128]{1,0:T(8,128)(2,1)S(1)} %get-tuple-element.34), channel_id=1, source_target_pairs={{1,0},{2,1},{3,2},{4,3},{5,4},{6,5},{7,6},{9,8},{10,9},{11,10},{12... | collective-permute-start | bytes 528392 | tf_op jit(solution)/shard_map/ppermute | solution.py:480
  29.0 3.0 %collective-permute-start.2 = (bf16[688,128]{1,0:T(8,128)(2,1)S(1)}, bf16[688,128]{1,0:T(8,128)(2,1)S(1)}, u32[]{:S(2)}, u32[]{:S(2)}) collective-permute-start(bf16[688,128]{1,0:T(8,128)(2,1)S(1)} %get-tuple-element.35), channel_id=1, source_target_pairs={{0,1},{1,2},{2,3},{3,4},{4,5},{5,6},{6,7},{8,9},{9,10},{10,11},{11... | collective-permute-start | bytes 528392 | tf_op jit(solution)/shard_map/ppermute | solution.py:480
  32.7 0.8 collective-permute-done.3.upper
  33.5 0.9 collective-permute-done.2.lower
  35.2 33.1 %forward.1 = (bf16[10,10,5,16,256]{4,3,2,1,0:T(8,128)(2,1)}, bf16[528,128]{1,0:T(8,128)(2,1)}, bf16[528,128]{1,0:T(8,128)(2,1)}, bf16[528,128]{1,0:T(8,128)(2,1)...) custom-call(bf16[16,512,128]{2,1,0:T(8,128)(2,1)} %bitcast.27, ...), custom_call_target="tpu_custom_call" | custom-call | flops 37399998464 | bytes 1048576 | tf_op jit(solution)/shard_map/forward/pallas_call | solution.py:532
  68.4 6.2 %all-to-all-start.1 = ((bf16[8,640,128]{2,1,0:T(8,128)(2,1)}), bf16[8,640,128]{2,1,0:T(8,128)(2,1)S(1)}, u32[]{:S(2)}, u32[]{:S(2)}) async-start(bf16[8,640,128]{2,1,0:T(8,128)(2,1)} %bitcast.18), calls=%async_computation.1 | async-start | bytes 2621440 | tf_op jit(solution)/shard_map/all_to_all | solution.py:562
  74.7 3.3 %collective-permute-start.4 = (bf16[528,128]{1,0:T(8,128)(2,1)S(1)}, bf16[528,128]{1,0:T(8,128)(2,1)S(1)}, u32[]{:S(2)}, u32[]{:S(2)}) collective-permute-start(bf16[528,128]{1,0:T(8,128)(2,1)S(1)} %copy-done.14), channel_id=1, source_target_pairs={{0,8},{8,16},{16,24},{24,32},{32,40},{40,48},{48,56},{56,64},{64,7... | collective-permute-start | bytes 405512 | tf_op jit(solution)/shard_map/ppermute | solution.py:480
  78.0 1.3 collective-permute-start.5
  79.3 1.6 %collective-permute-done.4.left = bf16[528,128]{1,0:T(8,128)(2,1)S(1)} collective-permute-done((bf16[528,128]{1,0:T(8,128)(2,1)S(1)}, bf16[528,128]{1,0:T(8,128)(2,1)S(1)}, u32[]{:S(2)}, u32[]{:S(2)}) %collective-permute-start.4) | collective-permute-done | bytes 135200 | tf_op jit(solution)/shard_map/ppermute | solution.py:480
  81.0 11.6 %all-to-all-done.1 = bf16[8,640,128]{2,1,0:T(8,128)(2,1)S(1)} async-done(((bf16[8,640,128]{2,1,0:T(8,128)(2,1)}), bf16[8,640,128]{2,1,0:T(8,128)(2,1)S(1)}, u32[]{:S(2)}, u32[]{:S(2)}) %all-to-all-start.1) | async-done | bytes 1310752 | tf_op jit(solution)/shard_map/all_to_all | solution.py:562
  92.8 0.9 pad_maximum_fusion
  93.7 6.6 %all-to-all-start.2 = ((bf16[16,168,128]{2,1,0:T(8,128)(2,1)}), bf16[16,168,128]{2,1,0:T(8,128)(2,1)S(1)}, u32[]{:S(2)}, u32[]{:S(2)}) async-start(bf16[16,168,128]{2,1,0:T(8,128)(2,1)} %pad_maximum_fusion), calls=%async_computation.2 | async-start | bytes 1376256 | tf_op jit(solution)/shard_map/all_to_all | solution.py:584
  100.3 3.1 %collective-permute-start.7 = (bf16[688,128]{1,0:T(8,128)(2,1)S(1)}, bf16[688,128]{1,0:T(8,128)(2,1)S(1)}, u32[]{:S(2)}, u32[]{:S(2)}) collective-permute-start(bf16[688,128]{1,0:T(8,128)(2,1)S(1)} %get-tuple-element.26), channel_id=1, source_target_pairs={{1,0},{2,1},{3,2},{4,3},{5,4},{6,5},{7,6},{9,8},{10,9},{11,10},{12... | collective-permute-start | bytes 528392 | tf_op jit(solution)/shard_map/ppermute | solution.py:480
  103.4 2.5 %collective-permute-start.6 = (bf16[688,128]{1,0:T(8,128)(2,1)S(1)}, bf16[688,128]{1,0:T(8,128)(2,1)S(1)}, u32[]{:S(2)}, u32[]{:S(2)}) collective-permute-start(bf16[688,128]{1,0:T(8,128)(2,1)S(1)} %get-tuple-element.27), channel_id=1, source_target_pairs={{0,1},{1,2},{2,3},{3,4},{4,5},{5,6},{6,7},{8,9},{9,10},{10,11},{11... | collective-permute-start | bytes 528392 | tf_op jit(solution)/shard_map/ppermute | solution.py:480
  105.9 0.8 reshape.45.mask_rows
  106.7 5.5 %all-to-all-done.2 = bf16[16,168,128]{2,1,0:T(8,128)(2,1)S(1)} async-done(((bf16[16,168,128]{2,1,0:T(8,128)(2,1)}), bf16[16,168,128]{2,1,0:T(8,128)(2,1)S(1)}, u32[]{:S(2)}, u32[]{:S(2)}) %all-to-all-start.2) | async-done | bytes 688160 | tf_op jit(solution)/shard_map/all_to_all | solution.py:584
  112.2 1.2 broadcast_in_dim.10
  113.4 5.8 %all-to-all-start.3 = ((bf16[128,40,128]{2,1,0:T(8,128)(2,1)}), bf16[128,40,128]{2,1,0:T(8,128)(2,1)S(1)}, u32[]{:S(2)}, u32[]{:S(2)}) async-start(bf16[128,40,128]{2,1,0:T(8,128)(2,1)} %broadcast_in_dim.10), calls=%async_computation.3 | async-start | bytes 2621440 | tf_op jit(solution)/shard_map/all_to_all | solution.py:587
  120.0 19.5 %backward.1 = bf16[16,512,128]{2,1,0:T(8,128)(2,1)} custom-call(bf16[10,10,5,16,256]{4,3,2,1,0:T(8,128)(2,1)} %get-tuple-element.21.grad_in, bf16[8,4,256]{2,1,0:T(4,128)(2,1)} %reshape.45.mask_rows, bf16[528,128]{1,0:T(8,128)(2,1)} %copy-done.4, bf16[528,128]{1,0:T(8,128)(2,1)} %copy-done.5, bf16[688,128]{1,0:T(8,128)(2,1)} %copy-done.10, ...), custom_call_target="tpu_custom_call" | custom-call | flops 19800000512 | bytes 1048576 | tf_op jit(solution)/shard_map/backward/pallas_call | solution.py:563
  139.5 0.8 slice.70
  140.6 0.8 convert_multiply_fusion.1
  141.5 1.3 convert_multiply_fusion
  (52 shorter events, 4.7 us)
Async XLA Ops:
  6.1 6.9 %collective-permute-start = (bf16[528,128]{1,0:T(8,128)(2,1)}, bf16[528,128]{1,0:T(8,128)(2,1)S(1)}, u32[]{:S(2)}, u32[]{:S(2)}) collective-permute-start(bf16[528,128]{1,0:T(8,128)(2,1)} %get-tuple-element.15), channel_id=1, source_target_pairs={{0,8},{8,16},{16,24},{24,32},{32,40},{40,48},{48,56},{56,64},{64,7... | collective-permute-start | bytes 405512 | tf_op jit(solution)/shard_map/ppermute | solution.py:480
  10.5 14.1 %collective-permute-start.1 = (bf16[528,128]{1,0:T(8,128)(2,1)}, bf16[528,128]{1,0:T(8,128)(2,1)S(1)}, u32[]{:S(2)}, u32[]{:S(2)}) collective-permute-start(bf16[528,128]{1,0:T(8,128)(2,1)} %get-tuple-element.16), channel_id=1, source_target_pairs={{8,0},{16,8},{24,16},{32,24},{40,32},{48,40},{56,48},{64,56},{72,6... | collective-permute-start | bytes 405512 | tf_op jit(solution)/shard_map/ppermute | solution.py:480
  13.0 0.7 copy-start.6
  13.7 18.4 %copy-start.8 = (s32[1,1,16,2]{2,3,1,0:T(2,128)S(1)}, s32[1,1,16,2]{2,3,1,0:T(2,128)}, u32[]{:S(2)}) copy-start(s32[1,1,16,2]{2,3,1,0:T(2,128)} %param.12) | copy-start | bytes 388
  15.5 18.9 %all-to-all-start = ((bf16[16,128,128]{2,1,0:T(8,128)(2,1)}), bf16[16,128,128]{2,1,0:T(8,128)(2,1)S(1)}, u32[]{:S(2)}, u32[]{:S(2)}) async-start(bf16[16,128,128]{2,1,0:T(8,128)(2,1)} %later.1), calls=%async_computation | async-start | bytes 1048576 | tf_op jit(solution)/shard_map/all_to_all | solution.py:528
  24.5 9.9 %copy-start.7 = (bf16[528,128]{1,0:T(8,128)(2,1)}, bf16[528,128]{1,0:T(8,128)(2,1)S(1)}, u32[]{:S(2)}) copy-start(bf16[528,128]{1,0:T(8,128)(2,1)S(1)} %collective-permute-done.1.right) | copy-start | bytes 405508
  25.3 8.2 %collective-permute-start.3 = (bf16[688,128]{1,0:T(8,128)(2,1)S(1)}, bf16[688,128]{1,0:T(8,128)(2,1)S(1)}, u32[]{:S(2)}, u32[]{:S(2)}) collective-permute-start(bf16[688,128]{1,0:T(8,128)(2,1)S(1)} %get-tuple-element.34), channel_id=1, source_target_pairs={{1,0},{2,1},{3,2},{4,3},{5,4},{6,5},{7,6},{9,8},{10,9},{11,10},{12... | collective-permute-start | bytes 528392 | tf_op jit(solution)/shard_map/ppermute | solution.py:480
  29.0 5.4 %collective-permute-start.2 = (bf16[688,128]{1,0:T(8,128)(2,1)S(1)}, bf16[688,128]{1,0:T(8,128)(2,1)S(1)}, u32[]{:S(2)}, u32[]{:S(2)}) collective-permute-start(bf16[688,128]{1,0:T(8,128)(2,1)S(1)} %get-tuple-element.35), channel_id=1, source_target_pairs={{0,1},{1,2},{2,3},{3,4},{4,5},{5,6},{6,7},{8,9},{9,10},{10,11},{11... | collective-permute-start | bytes 528392 | tf_op jit(solution)/shard_map/ppermute | solution.py:480
  33.5 0.9 copy-start.11
  34.4 0.7 copy-start.12
  34.4 0.8 copy-start
  68.4 6.2 %copy-start.14 = (bf16[528,128]{1,0:T(8,128)(2,1)S(1)}, bf16[528,128]{1,0:T(8,128)(2,1)}, u32[]{:S(2)}) copy-start(bf16[528,128]{1,0:T(8,128)(2,1)} %get-tuple-element.22) | copy-start | bytes 405508
  68.4 9.6 %copy-start.13 = (bf16[528,128]{1,0:T(8,128)(2,1)S(1)}, bf16[528,128]{1,0:T(8,128)(2,1)}, u32[]{:S(2)}) copy-start(bf16[528,128]{1,0:T(8,128)(2,1)} %get-tuple-element.23) | copy-start | bytes 405508
  68.4 10.9 %copy-start.3 = (bf16[528,128]{1,0:T(8,128)(2,1)S(1)}, bf16[528,128]{1,0:T(8,128)(2,1)}, u32[]{:S(2)}) copy-start(bf16[528,128]{1,0:T(8,128)(2,1)} %get-tuple-element.24) | copy-start | bytes 405508
  68.4 10.9 %copy-start.2 = (bf16[528,128]{1,0:T(8,128)(2,1)S(1)}, bf16[528,128]{1,0:T(8,128)(2,1)}, u32[]{:S(2)}) copy-start(bf16[528,128]{1,0:T(8,128)(2,1)} %get-tuple-element.25) | copy-start | bytes 405508
  68.4 24.1 %all-to-all-start.1 = ((bf16[8,640,128]{2,1,0:T(8,128)(2,1)}), bf16[8,640,128]{2,1,0:T(8,128)(2,1)S(1)}, u32[]{:S(2)}, u32[]{:S(2)}) async-start(bf16[8,640,128]{2,1,0:T(8,128)(2,1)} %bitcast.18), calls=%async_computation.1 | async-start | bytes 2621440 | tf_op jit(solution)/shard_map/all_to_all | solution.py:562
  74.6 18.1 %copy-start.1 = (bf16[32,64,128]{2,1,0:T(8,128)(2,1)S(1)}, bf16[32,64,128]{2,1,0:T(8,128)(2,1)}, u32[]{:S(2)}) copy-start(bf16[32,64,128]{2,1,0:T(8,128)(2,1)} %get-tuple-element.19) | copy-start | bytes 1572868
  74.7 6.3 %collective-permute-start.4 = (bf16[528,128]{1,0:T(8,128)(2,1)S(1)}, bf16[528,128]{1,0:T(8,128)(2,1)S(1)}, u32[]{:S(2)}, u32[]{:S(2)}) collective-permute-start(bf16[528,128]{1,0:T(8,128)(2,1)S(1)} %copy-done.14), channel_id=1, source_target_pairs={{0,8},{8,16},{16,24},{24,32},{32,40},{40,48},{48,56},{56,64},{64,7... | collective-permute-start | bytes 405512 | tf_op jit(solution)/shard_map/ppermute | solution.py:480
  78.0 22.3 %collective-permute-start.5 = (bf16[528,128]{1,0:T(8,128)(2,1)S(1)}, bf16[528,128]{1,0:T(8,128)(2,1)S(1)}, u32[]{:S(2)}, u32[]{:S(2)}) collective-permute-start(bf16[528,128]{1,0:T(8,128)(2,1)S(1)} %copy-done.13), channel_id=1, source_target_pairs={{8,0},{16,8},{24,16},{32,24},{40,32},{48,40},{56,48},{64,56},{72,6... | collective-permute-start | bytes 405512 | tf_op jit(solution)/shard_map/ppermute | solution.py:480
  80.9 19.3 %copy-start.4 = (bf16[528,128]{1,0:T(8,128)(2,1)}, bf16[528,128]{1,0:T(8,128)(2,1)S(1)}, u32[]{:S(2)}) copy-start(bf16[528,128]{1,0:T(8,128)(2,1)S(1)} %collective-permute-done.4.left) | copy-start | bytes 405508
  93.7 18.5 %all-to-all-start.2 = ((bf16[16,168,128]{2,1,0:T(8,128)(2,1)}), bf16[16,168,128]{2,1,0:T(8,128)(2,1)S(1)}, u32[]{:S(2)}, u32[]{:S(2)}) async-start(bf16[16,168,128]{2,1,0:T(8,128)(2,1)} %pad_maximum_fusion), calls=%async_computation.2 | async-start | bytes 1376256 | tf_op jit(solution)/shard_map/all_to_all | solution.py:584
  100.2 13.2 %copy-start.5 = (bf16[528,128]{1,0:T(8,128)(2,1)}, bf16[528,128]{1,0:T(8,128)(2,1)S(1)}, u32[]{:S(2)}) copy-start(bf16[528,128]{1,0:T(8,128)(2,1)S(1)} %collective-permute-done.5.right) | copy-start | bytes 405508
  100.3 19.0 %collective-permute-start.7 = (bf16[688,128]{1,0:T(8,128)(2,1)S(1)}, bf16[688,128]{1,0:T(8,128)(2,1)S(1)}, u32[]{:S(2)}, u32[]{:S(2)}) collective-permute-start(bf16[688,128]{1,0:T(8,128)(2,1)S(1)} %get-tuple-element.26), channel_id=1, source_target_pairs={{1,0},{2,1},{3,2},{4,3},{5,4},{6,5},{7,6},{9,8},{10,9},{11,10},{12... | collective-permute-start | bytes 528392 | tf_op jit(solution)/shard_map/ppermute | solution.py:480
  103.4 15.9 %collective-permute-start.6 = (bf16[688,128]{1,0:T(8,128)(2,1)S(1)}, bf16[688,128]{1,0:T(8,128)(2,1)S(1)}, u32[]{:S(2)}, u32[]{:S(2)}) collective-permute-start(bf16[688,128]{1,0:T(8,128)(2,1)S(1)} %get-tuple-element.27), channel_id=1, source_target_pairs={{0,1},{1,2},{2,3},{3,4},{4,5},{5,6},{6,7},{8,9},{9,10},{10,11},{11... | collective-permute-start | bytes 528392 | tf_op jit(solution)/shard_map/ppermute | solution.py:480
  113.4 27.2 %all-to-all-start.3 = ((bf16[128,40,128]{2,1,0:T(8,128)(2,1)}), bf16[128,40,128]{2,1,0:T(8,128)(2,1)S(1)}, u32[]{:S(2)}, u32[]{:S(2)}) async-start(bf16[128,40,128]{2,1,0:T(8,128)(2,1)} %broadcast_in_dim.10), calls=%async_computation.3 | async-start | bytes 2621440 | tf_op jit(solution)/shard_map/all_to_all | solution.py:587
  119.3 0.7 copy-start.9
  119.3 0.7 copy-start.10

commit v4 on v3

--- a/solution.py
+++ b/solution.py
@@ -207,10 +207,10 @@
     own = jnp.full((1, 128), NOWHERE, jnp.int32)
     target_row = jnp.full((1, 128), NOWHERE, jnp.int32)
     for s in range(SLOTS):
-        x, y, z = (coord[0, 0, s, d] for d in range(3))
+        x, y, z = (coord[d, s] for d in range(3))
         live = (s if s < BORDER else s - BORDER) < count[0, 0, 0 if s < BORDER else 1]
         code = position_code(x, y, z)
-        place = jnp.where(live, routes[0, 0, s, 0] * CAP + routes[0, 0, s, 1], NOWHERE)
+        place = jnp.where(live, routes[0, s] * CAP + routes[1, s], NOWHERE)
         base = jnp.where(sub == s, code, base)
         target = jnp.where(sub == s, place, target)
         own = jnp.where(lane % SLOTS == s, jnp.where(live, code, NOWHERE), own)
@@ -222,7 +222,7 @@
     lane = lane_row()
     row = jnp.zeros((1, 128), jnp.int32)
     for s in range(BORDER):
-        x, y, z = (coord[0, 0, s, d] for d in range(3))
+        x, y, z = (coord[d, s] for d in range(3))
         label = jnp.where(s < count[0, 0, 0], 1 + x + TILE * y + TILE * TILE * z, 0)
         row = jnp.where(lane % BORDER == s, label, row)
     rows = jnp.broadcast_to(row.astype(F32), (LAB, 128)).astype(BF)
@@ -501,7 +501,7 @@
     mask_rows = active.reshape(SLOTS, EDGE, 4, 16).transpose(1, 2, 0, 3).reshape(EDGE, 4, 256)
     by_pair = active.reshape(SLOTS, EDGE, 4, 2, 4, 2)
     back_rows = by_pair.transpose(1, 2, 5, 3, 4, 0).reshape(EDGE, 4, 256)
-    scalars = (brick_coord, brick_count, route)
+    scalars = (brick_coord[0, 0].T, brick_count, route[0, 0].T)
 
     face = jax.ShapeDtypeStruct((XMSG, CH), BF)
     volume = jax.ShapeDtypeStruct(VOLUME, BF)
@@ -519,7 +519,7 @@
     cotangents = pl.pallas_call(
         later_kernel,
         out_shape=jax.ShapeDtypeStruct((tiles_x, CAP * 64, CH), BF),
-        in_specs=whole(1) + [pl.BlockSpec(memory_space=pl.ANY)],
+        in_specs=whole(2),
         out_specs=whole(1)[0],
         compiler_params=pltpu.CompilerParams(vmem_limit_bytes=VMEM_LIMIT),
         cost_estimate=microseconds(1),

time: 144 us -> 144 us (level)
    unnamed x42 -> x39, local copies, waits for them, and re-layouts: 7.65 us -> 6.9 us
where the time goes in v4:
time: 144 us; the launch traced here: 143 us
  Pallas kernels  56.8 us (39%)
  starting transfers between devices  49.4 us (34%)
  waiting for transfers between devices  21.6 us (15%)
  local copies, waits for them, and re-layouts  10.7 us (7%)
  other arithmetic  3.31 us (2%)
    pallas_call x1, Pallas kernels, per_device(): pl.pallas_call(forward_kernel, out_shape=(volume,) + (face,) * 4 + (jax.S...  33.1 us
    ppermute x8, starting transfers between devices, shift(): return lax.ppermute(value, axis, pairs)  22.6 us
    pallas_call x1, Pallas kernels, per_device(): pl.pallas_call(backward_kernel, out_shape=jax.ShapeDtypeStruct((SLOTS, VO...  19.5 us
    all_to_all x1, waiting for transfers between devices, per_device(): lax.all_to_all(partial.reshape(tiles_y, shares, CH), 'gy', 0, 0, tiled=True)  11.6 us
    all_to_all x1, starting transfers between devices, per_device(): lax.all_to_all(cotangents, 'gx', 0, 0, tiled=True)  8.22 us
    unnamed x39, local copies, waits for them, and re-layouts  6.9 us
    all_to_all x1, starting transfers between devices, per_device(): parts = lax.all_to_all(message, 'gx', 0, 0, tiled=True)  6.56 us
    all_to_all x1, starting transfers between devices, per_device(): lax.all_to_all(partial.reshape(tiles_y, shares, CH), 'gy', 0, 0, tiled=True)  6.2 us
  transfers between devices with their start and end apart: 12, of which 7 were waited for; matrix products, arithmetic and copies ran while one was open for 5% of the time, Pallas kernels for 15%

profile of v4, /device:TPU:1, one launch (start us, length us, event | category | flops | bytes accessed | tf_op | source)
XLA Modules:
  0.0 142.7 jit_solution(9084337732678187875)
XLA Ops:
  0.6 1.3 copy.19
  1.9 0.9 copy.14
  2.9 0.8 reshape.39.mask_rows
  3.7 2.3 %faces.1 = (bf16[528,128]{1,0:T(8,128)(2,1)}, bf16[528,128]{1,0:T(8,128)(2,1)}, bf16[528,128]{1,0:T(8,128)(2,1)}, bf16[528,128]{1,0:T(8,128)(2,1)}) custom-call(bf16[16,512,128]{2,1,0:T(8,128)(2,1)} %bitcast.37, bf16[8,4,256]{2,1,0:T(4,128)(2,1)} %reshape.39.mask_rows, s32[3,16]{1,0:T(4,128)} %bitcast.34, s32[1,1,2]{2,1,0:T(1,128)} %count.5), custom_call_target="tpu_custom_call" | custom-call | flops 2200000000 | bytes 1048576 | tf_op jit(solution)/shard_map/faces/pallas_call | solution.py:508
  6.0 4.4 %collective-permute-start = (bf16[528,128]{1,0:T(8,128)(2,1)}, bf16[528,128]{1,0:T(8,128)(2,1)S(1)}, u32[]{:S(2)}, u32[]{:S(2)}) collective-permute-start(bf16[528,128]{1,0:T(8,128)(2,1)} %get-tuple-element.15), channel_id=1, source_target_pairs={{0,8},{8,16},{16,24},{24,32},{32,40},{40,48},{48,56},{56,64},{64,7... | collective-permute-start | bytes 405512 | tf_op jit(solution)/shard_map/ppermute | solution.py:480
  10.4 1.3 collective-permute-start.1
  11.7 1.0 constant_dynamic-update-slice_fusion.4
  13.6 1.9 %later.1 = bf16[16,128,128]{2,1,0:T(8,128)(2,1)} custom-call(bf16[16,128,128]{2,1,0:T(8,128)(2,1)} %bitcast.39, bf16[528,128]{1,0:T(8,128)(2,1)} %copy-done.6), custom_call_target="tpu_custom_call" | custom-call | flops 1100000000 | bytes 1048576 | tf_op jit(solution)/shard_map/later/pallas_call | solution.py:519
  15.5 8.2 %all-to-all-start = ((bf16[16,128,128]{2,1,0:T(8,128)(2,1)}), bf16[16,128,128]{2,1,0:T(8,128)(2,1)S(1)}, u32[]{:S(2)}, u32[]{:S(2)}) async-start(bf16[16,128,128]{2,1,0:T(8,128)(2,1)} %later.1), calls=%async_computation | async-start | bytes 1048576 | tf_op jit(solution)/shard_map/all_to_all | solution.py:528
  23.7 0.7 constant_dynamic-update-slice_fusion.8
  25.2 3.7 %collective-permute-start.3 = (bf16[688,128]{1,0:T(8,128)(2,1)S(1)}, bf16[688,128]{1,0:T(8,128)(2,1)S(1)}, u32[]{:S(2)}, u32[]{:S(2)}) collective-permute-start(bf16[688,128]{1,0:T(8,128)(2,1)S(1)} %get-tuple-element.34), channel_id=1, source_target_pairs={{1,0},{2,1},{3,2},{4,3},{5,4},{6,5},{7,6},{9,8},{10,9},{11,10},{12... | collective-permute-start | bytes 528392 | tf_op jit(solution)/shard_map/ppermute | solution.py:480
  28.9 3.0 %collective-permute-start.2 = (bf16[688,128]{1,0:T(8,128)(2,1)S(1)}, bf16[688,128]{1,0:T(8,128)(2,1)S(1)}, u32[]{:S(2)}, u32[]{:S(2)}) collective-permute-start(bf16[688,128]{1,0:T(8,128)(2,1)S(1)} %get-tuple-element.35), channel_id=1, source_target_pairs={{0,1},{1,2},{2,3},{3,4},{4,5},{5,6},{6,7},{8,9},{9,10},{10,11},{11... | collective-permute-start | bytes 528392 | tf_op jit(solution)/shard_map/ppermute | solution.py:480
  32.0 1.5 %collective-permute-done.3.upper = bf16[688,128]{1,0:T(8,128)(2,1)S(1)} collective-permute-done((bf16[688,128]{1,0:T(8,128)(2,1)S(1)}, bf16[688,128]{1,0:T(8,128)(2,1)S(1)}, u32[]{:S(2)}, u32[]{:S(2)}) %collective-permute-start.3) | collective-permute-done | bytes 176160 | tf_op jit(solution)/shard_map/ppermute | solution.py:480
  33.5 0.9 collective-permute-done.2.lower
  35.2 33.1 %forward.1 = (bf16[10,10,5,16,256]{4,3,2,1,0:T(8,128)(2,1)}, bf16[528,128]{1,0:T(8,128)(2,1)}, bf16[528,128]{1,0:T(8,128)(2,1)}, bf16[528,128]{1,0:T(8,128)(2,1)...) custom-call(bf16[16,512,128]{2,1,0:T(8,128)(2,1)} %bitcast.38, ...), custom_call_target="tpu_custom_call" | custom-call | flops 37399998464 | bytes 1048576 | tf_op jit(solution)/shard_map/forward/pallas_call | solution.py:532
  68.4 6.2 %all-to-all-start.1 = ((bf16[8,640,128]{2,1,0:T(8,128)(2,1)}), bf16[8,640,128]{2,1,0:T(8,128)(2,1)S(1)}, u32[]{:S(2)}, u32[]{:S(2)}) async-start(bf16[8,640,128]{2,1,0:T(8,128)(2,1)} %bitcast.26), calls=%async_computation.1 | async-start | bytes 2621440 | tf_op jit(solution)/shard_map/all_to_all | solution.py:562
  74.6 3.3 %collective-permute-start.4 = (bf16[528,128]{1,0:T(8,128)(2,1)S(1)}, bf16[528,128]{1,0:T(8,128)(2,1)S(1)}, u32[]{:S(2)}, u32[]{:S(2)}) collective-permute-start(bf16[528,128]{1,0:T(8,128)(2,1)S(1)} %copy-done.13), channel_id=1, source_target_pairs={{0,8},{8,16},{16,24},{24,32},{32,40},{40,48},{48,56},{56,64},{64,7... | collective-permute-start | bytes 405512 | tf_op jit(solution)/shard_map/ppermute | solution.py:480
  77.9 1.3 collective-permute-start.5
  79.3 1.6 %collective-permute-done.4.left = bf16[528,128]{1,0:T(8,128)(2,1)S(1)} collective-permute-done((bf16[528,128]{1,0:T(8,128)(2,1)S(1)}, bf16[528,128]{1,0:T(8,128)(2,1)S(1)}, u32[]{:S(2)}, u32[]{:S(2)}) %collective-permute-start.4) | collective-permute-done | bytes 135200 | tf_op jit(solution)/shard_map/ppermute | solution.py:480
  80.9 11.6 %all-to-all-done.1 = bf16[8,640,128]{2,1,0:T(8,128)(2,1)S(1)} async-done(((bf16[8,640,128]{2,1,0:T(8,128)(2,1)}), bf16[8,640,128]{2,1,0:T(8,128)(2,1)S(1)}, u32[]{:S(2)}, u32[]{:S(2)}) %all-to-all-start.1) | async-done | bytes 1310752 | tf_op jit(solution)/shard_map/all_to_all | solution.py:562
  92.7 0.9 pad_maximum_fusion
  93.6 6.6 %all-to-all-start.2 = ((bf16[16,168,128]{2,1,0:T(8,128)(2,1)}), bf16[16,168,128]{2,1,0:T(8,128)(2,1)S(1)}, u32[]{:S(2)}, u32[]{:S(2)}) async-start(bf16[16,168,128]{2,1,0:T(8,128)(2,1)} %pad_maximum_fusion), calls=%async_computation.2 | async-start | bytes 1376256 | tf_op jit(solution)/shard_map/all_to_all | solution.py:584
  100.2 3.1 %collective-permute-start.7 = (bf16[688,128]{1,0:T(8,128)(2,1)S(1)}, bf16[688,128]{1,0:T(8,128)(2,1)S(1)}, u32[]{:S(2)}, u32[]{:S(2)}) collective-permute-start(bf16[688,128]{1,0:T(8,128)(2,1)S(1)} %get-tuple-element.26), channel_id=1, source_target_pairs={{1,0},{2,1},{3,2},{4,3},{5,4},{6,5},{7,6},{9,8},{10,9},{11,10},{12... | collective-permute-start | bytes 528392 | tf_op jit(solution)/shard_map/ppermute | solution.py:480
  103.3 2.5 %collective-permute-start.6 = (bf16[688,128]{1,0:T(8,128)(2,1)S(1)}, bf16[688,128]{1,0:T(8,128)(2,1)S(1)}, u32[]{:S(2)}, u32[]{:S(2)}) collective-permute-start(bf16[688,128]{1,0:T(8,128)(2,1)S(1)} %get-tuple-element.27), channel_id=1, source_target_pairs={{0,1},{1,2},{2,3},{3,4},{4,5},{5,6},{6,7},{8,9},{9,10},{10,11},{11... | collective-permute-start | bytes 528392 | tf_op jit(solution)/shard_map/ppermute | solution.py:480
  105.9 0.8 reshape.45.mask_rows
  106.6 5.5 %all-to-all-done.2 = bf16[16,168,128]{2,1,0:T(8,128)(2,1)S(1)} async-done(((bf16[16,168,128]{2,1,0:T(8,128)(2,1)}), bf16[16,168,128]{2,1,0:T(8,128)(2,1)S(1)}, u32[]{:S(2)}, u32[]{:S(2)}) %all-to-all-start.2) | async-done | bytes 688160 | tf_op jit(solution)/shard_map/all_to_all | solution.py:584
  112.1 1.2 broadcast_in_dim.10
  113.4 5.8 %all-to-all-start.3 = ((bf16[128,40,128]{2,1,0:T(8,128)(2,1)}), bf16[128,40,128]{2,1,0:T(8,128)(2,1)S(1)}, u32[]{:S(2)}, u32[]{:S(2)}) async-start(bf16[128,40,128]{2,1,0:T(8,128)(2,1)} %broadcast_in_dim.10), calls=%async_computation.3 | async-start | bytes 2621440 | tf_op jit(solution)/shard_map/all_to_all | solution.py:587
  120.0 19.5 %backward.1 = bf16[16,512,128]{2,1,0:T(8,128)(2,1)} custom-call(bf16[10,10,5,16,256]{4,3,2,1,0:T(8,128)(2,1)} %get-tuple-element.21.grad_in, bf16[8,4,256]{2,1,0:T(4,128)(2,1)} %reshape.45.mask_rows, bf16[528,128]{1,0:T(8,128)(2,1)} %copy-done.4, bf16[528,128]{1,0:T(8,128)(2,1)} %copy-done.5, bf16[688,128]{1,0:T(8,128)(2,1)} %copy-done.9, ...), custom_call_target="tpu_custom_call" | custom-call | flops 19800000512 | bytes 1048576 | tf_op jit(solution)/shard_map/backward/pallas_call | solution.py:563
  139.4 0.8 slice.70
  140.6 0.8 convert_multiply_fusion.1
  141.4 1.3 convert_multiply_fusion
  (49 shorter events, 4.0 us)
Async XLA Ops:
  6.0 6.9 %collective-permute-start = (bf16[528,128]{1,0:T(8,128)(2,1)}, bf16[528,128]{1,0:T(8,128)(2,1)S(1)}, u32[]{:S(2)}, u32[]{:S(2)}) collective-permute-start(bf16[528,128]{1,0:T(8,128)(2,1)} %get-tuple-element.15), channel_id=1, source_target_pairs={{0,8},{8,16},{16,24},{24,32},{32,40},{40,48},{48,56},{56,64},{64,7... | collective-permute-start | bytes 405512 | tf_op jit(solution)/shard_map/ppermute | solution.py:480
  10.4 14.1 %collective-permute-start.1 = (bf16[528,128]{1,0:T(8,128)(2,1)}, bf16[528,128]{1,0:T(8,128)(2,1)S(1)}, u32[]{:S(2)}, u32[]{:S(2)}) collective-permute-start(bf16[528,128]{1,0:T(8,128)(2,1)} %get-tuple-element.16), channel_id=1, source_target_pairs={{8,0},{16,8},{24,16},{32,24},{40,32},{48,40},{56,48},{64,56},{72,6... | collective-permute-start | bytes 405512 | tf_op jit(solution)/shard_map/ppermute | solution.py:480
  12.9 0.7 copy-start.6
  15.5 18.9 %all-to-all-start = ((bf16[16,128,128]{2,1,0:T(8,128)(2,1)}), bf16[16,128,128]{2,1,0:T(8,128)(2,1)S(1)}, u32[]{:S(2)}, u32[]{:S(2)}) async-start(bf16[16,128,128]{2,1,0:T(8,128)(2,1)} %later.1), calls=%async_computation | async-start | bytes 1048576 | tf_op jit(solution)/shard_map/all_to_all | solution.py:528
  24.5 9.9 %copy-start.7 = (bf16[528,128]{1,0:T(8,128)(2,1)}, bf16[528,128]{1,0:T(8,128)(2,1)S(1)}, u32[]{:S(2)}) copy-start(bf16[528,128]{1,0:T(8,128)(2,1)S(1)} %collective-permute-done.1.right) | copy-start | bytes 405508
  25.2 8.2 %collective-permute-start.3 = (bf16[688,128]{1,0:T(8,128)(2,1)S(1)}, bf16[688,128]{1,0:T(8,128)(2,1)S(1)}, u32[]{:S(2)}, u32[]{:S(2)}) collective-permute-start(bf16[688,128]{1,0:T(8,128)(2,1)S(1)} %get-tuple-element.34), channel_id=1, source_target_pairs={{1,0},{2,1},{3,2},{4,3},{5,4},{6,5},{7,6},{9,8},{10,9},{11,10},{12... | collective-permute-start | bytes 528392 | tf_op jit(solution)/shard_map/ppermute | solution.py:480
  28.9 5.4 %collective-permute-start.2 = (bf16[688,128]{1,0:T(8,128)(2,1)S(1)}, bf16[688,128]{1,0:T(8,128)(2,1)S(1)}, u32[]{:S(2)}, u32[]{:S(2)}) collective-permute-start(bf16[688,128]{1,0:T(8,128)(2,1)S(1)} %get-tuple-element.35), channel_id=1, source_target_pairs={{0,1},{1,2},{2,3},{3,4},{4,5},{5,6},{6,7},{8,9},{9,10},{10,11},{11... | collective-permute-start | bytes 528392 | tf_op jit(solution)/shard_map/ppermute | solution.py:480
  33.5 0.9 copy-start.10
  34.3 0.7 copy-start.11
  34.3 0.8 copy-start
  68.3 6.2 %copy-start.13 = (bf16[528,128]{1,0:T(8,128)(2,1)S(1)}, bf16[528,128]{1,0:T(8,128)(2,1)}, u32[]{:S(2)}) copy-start(bf16[528,128]{1,0:T(8,128)(2,1)} %get-tuple-element.22) | copy-start | bytes 405508
  68.4 9.6 %copy-start.12 = (bf16[528,128]{1,0:T(8,128)(2,1)S(1)}, bf16[528,128]{1,0:T(8,128)(2,1)}, u32[]{:S(2)}) copy-start(bf16[528,128]{1,0:T(8,128)(2,1)} %get-tuple-element.23) | copy-start | bytes 405508
  68.4 10.9 %copy-start.3 = (bf16[528,128]{1,0:T(8,128)(2,1)S(1)}, bf16[528,128]{1,0:T(8,128)(2,1)}, u32[]{:S(2)}) copy-start(bf16[528,128]{1,0:T(8,128)(2,1)} %get-tuple-element.24) | copy-start | bytes 405508
  68.4 10.9 %copy-start.2 = (bf16[528,128]{1,0:T(8,128)(2,1)S(1)}, bf16[528,128]{1,0:T(8,128)(2,1)}, u32[]{:S(2)}) copy-start(bf16[528,128]{1,0:T(8,128)(2,1)} %get-tuple-element.25) | copy-start | bytes 405508
  68.4 24.1 %all-to-all-start.1 = ((bf16[8,640,128]{2,1,0:T(8,128)(2,1)}), bf16[8,640,128]{2,1,0:T(8,128)(2,1)S(1)}, u32[]{:S(2)}, u32[]{:S(2)}) async-start(bf16[8,640,128]{2,1,0:T(8,128)(2,1)} %bitcast.26), calls=%async_computation.1 | async-start | bytes 2621440 | tf_op jit(solution)/shard_map/all_to_all | solution.py:562
  74.6 18.1 %copy-start.1 = (bf16[32,64,128]{2,1,0:T(8,128)(2,1)S(1)}, bf16[32,64,128]{2,1,0:T(8,128)(2,1)}, u32[]{:S(2)}) copy-start(bf16[32,64,128]{2,1,0:T(8,128)(2,1)} %get-tuple-element.19) | copy-start | bytes 1572868
  74.6 6.3 %collective-permute-start.4 = (bf16[528,128]{1,0:T(8,128)(2,1)S(1)}, bf16[528,128]{1,0:T(8,128)(2,1)S(1)}, u32[]{:S(2)}, u32[]{:S(2)}) collective-permute-start(bf16[528,128]{1,0:T(8,128)(2,1)S(1)} %copy-done.13), channel_id=1, source_target_pairs={{0,8},{8,16},{16,24},{24,32},{32,40},{40,48},{48,56},{56,64},{64,7... | collective-permute-start | bytes 405512 | tf_op jit(solution)/shard_map/ppermute | solution.py:480
  77.9 22.3 %collective-permute-start.5 = (bf16[528,128]{1,0:T(8,128)(2,1)S(1)}, bf16[528,128]{1,0:T(8,128)(2,1)S(1)}, u32[]{:S(2)}, u32[]{:S(2)}) collective-permute-start(bf16[528,128]{1,0:T(8,128)(2,1)S(1)} %copy-done.12), channel_id=1, source_target_pairs={{8,0},{16,8},{24,16},{32,24},{40,32},{48,40},{56,48},{64,56},{72,6... | collective-permute-start | bytes 405512 | tf_op jit(solution)/shard_map/ppermute | solution.py:480
  80.9 19.3 %copy-start.4 = (bf16[528,128]{1,0:T(8,128)(2,1)}, bf16[528,128]{1,0:T(8,128)(2,1)S(1)}, u32[]{:S(2)}) copy-start(bf16[528,128]{1,0:T(8,128)(2,1)S(1)} %collective-permute-done.4.left) | copy-start | bytes 405508
  93.6 18.5 %all-to-all-start.2 = ((bf16[16,168,128]{2,1,0:T(8,128)(2,1)}), bf16[16,168,128]{2,1,0:T(8,128)(2,1)S(1)}, u32[]{:S(2)}, u32[]{:S(2)}) async-start(bf16[16,168,128]{2,1,0:T(8,128)(2,1)} %pad_maximum_fusion), calls=%async_computation.2 | async-start | bytes 1376256 | tf_op jit(solution)/shard_map/all_to_all | solution.py:584
  100.2 13.2 %copy-start.5 = (bf16[528,128]{1,0:T(8,128)(2,1)}, bf16[528,128]{1,0:T(8,128)(2,1)S(1)}, u32[]{:S(2)}) copy-start(bf16[528,128]{1,0:T(8,128)(2,1)S(1)} %collective-permute-done.5.right) | copy-start | bytes 405508
  100.2 19.0 %collective-permute-start.7 = (bf16[688,128]{1,0:T(8,128)(2,1)S(1)}, bf16[688,128]{1,0:T(8,128)(2,1)S(1)}, u32[]{:S(2)}, u32[]{:S(2)}) collective-permute-start(bf16[688,128]{1,0:T(8,128)(2,1)S(1)} %get-tuple-element.26), channel_id=1, source_target_pairs={{1,0},{2,1},{3,2},{4,3},{5,4},{6,5},{7,6},{9,8},{10,9},{11,10},{12... | collective-permute-start | bytes 528392 | tf_op jit(solution)/shard_map/ppermute | solution.py:480
  103.3 15.9 %collective-permute-start.6 = (bf16[688,128]{1,0:T(8,128)(2,1)S(1)}, bf16[688,128]{1,0:T(8,128)(2,1)S(1)}, u32[]{:S(2)}, u32[]{:S(2)}) collective-permute-start(bf16[688,128]{1,0:T(8,128)(2,1)S(1)} %get-tuple-element.27), channel_id=1, source_target_pairs={{0,1},{1,2},{2,3},{3,4},{4,5},{5,6},{6,7},{8,9},{9,10},{10,11},{11... | collective-permute-start | bytes 528392 | tf_op jit(solution)/shard_map/ppermute | solution.py:480
  113.4 27.2 %all-to-all-start.3 = ((bf16[128,40,128]{2,1,0:T(8,128)(2,1)}), bf16[128,40,128]{2,1,0:T(8,128)(2,1)S(1)}, u32[]{:S(2)}, u32[]{:S(2)}) async-start(bf16[128,40,128]{2,1,0:T(8,128)(2,1)} %broadcast_in_dim.10), calls=%async_computation.3 | async-start | bytes 2621440 | tf_op jit(solution)/shard_map/all_to_all | solution.py:587
  119.2 0.7 copy-start.8
  119.3 0.7 copy-start.9
